TPU v7x, 512 devices: a whole 4x4x16 slice. The times are simulated.
512 devices in a mesh: rep: 4 (over x_lo, core), fsdp: 32 (over x_hi, z), tp: 4 (over y).
Axes of the slice: x: 4 (x_hi: 2, x_lo: 2; x = x_hi * 2 + x_lo), y: 4, z: 16, core: 2. Of those that a mesh axis runs over, the one named last changes fastest.
Arguments:
- inner_weights: bfloat16 [4, 8192, 8192], P('rep', 'fsdp', 'tp'), may hold values from -6 to 6
- outer_weights: float32 [32, 128, 2, 8192], P(None, ('rep', 'fsdp'), None, 'tp'), may hold values from -6 to 6
- outer_momentum: float32 [32, 128, 2, 8192], P(None, ('rep', 'fsdp'), None, 'tp'), may hold values from -6 to 6
Outputs:
- mixed_inner: bfloat16 [4, 8192, 8192], P('rep', 'fsdp', 'tp')
- new_outer: float32 [32, 128, 2, 8192], P(None, ('rep', 'fsdp'), None, 'tp')
- new_momentum: float32 [32, 128, 2, 8192], P(None, ('rep', 'fsdp'), None, 'tp')
All inputs are finite; a program needn't handle non-finite values.
Results may differ from a plain program's by a relative error of at most 0.0085.
Values may be sent and summed in bfloat16 or wider, within the bound.
No kernel may reach another device: no remote copies, remote signals or barrier semaphores. Data moves between devices by JAX's collectives and lax.ppermute only.
A program may use at most 64 MiB of HBM per device.

v0:
```python
import jax
import jax.numpy as jnp
from jax import lax
from jax.sharding import PartitionSpec as P


def on_device(inner_weights, outer_weights, outer_momentum):
    shard = inner_weights[0]
    rows_here, columns = shard.shape
    replicas = lax.axis_size("rep")
    blocks = lax.axis_size("fsdp")
    group = rows_here // (replicas * blocks)
    pieces = shard.reshape(replicas * blocks, group, columns)
    received = lax.all_to_all(pieces, ("rep", "fsdp"), split_axis=0, concat_axis=0, tiled=True)
    inner_total = jnp.sum(
        received.reshape(replicas, blocks, group, columns).astype(jnp.float32), axis=0
    )
    outer_here = outer_weights[:, 0]
    pseudo_grad = outer_here - inner_total / replicas
    new_momentum = 0.9 * outer_momentum[:, 0] + pseudo_grad
    new_outer = outer_here - 0.7 * (pseudo_grad + 0.9 * new_momentum)
    outer_copy = new_outer.astype(jnp.bfloat16)
    copies = lax.all_gather(outer_copy[None], "rep", axis=0, tiled=True)
    every_rows = lax.all_to_all(copies, "fsdp", split_axis=1, concat_axis=1, tiled=True)
    outer_rows = every_rows.reshape(rows_here, columns).astype(jnp.float32)
    mixed = (0.5 * shard.astype(jnp.float32) + 0.5 * outer_rows).astype(jnp.bfloat16)
    return (mixed[None], new_outer[:, None], new_momentum[:, None])


def solution(mesh):
    in_specs = (
        P("rep", "fsdp", "tp"),
        P(None, ("rep", "fsdp"), None, "tp"),
        P(None, ("rep", "fsdp"), None, "tp"),
    )
    out_specs = (
        P("rep", "fsdp", "tp"),
        P(None, ("rep", "fsdp"), None, "tp"),
        P(None, ("rep", "fsdp"), None, "tp"),
    )
    return jax.shard_map(
        on_device, mesh=mesh, in_specs=in_specs, out_specs=out_specs, check_vma=False
    )
```

profile of v0, /device:TPU:32, one launch (start us, length us, event | category | flops | bytes accessed | tf_op | source)
XLA Modules:
  0.0 195.5 jit_solution(12599410625178744684)
XLA Ops:
  7.2 0.0 all-gather.2.cloned.1.call-start
  7.2 1.7 reshape_squeeze.3
  9.0 0.0 copy-start.1
  9.0 0.0 copy-start.2
  9.0 74.9 %all_to_all.10 = bf16[128,2,2048]{2,1,0:T(2,128)(2,1)S(1)} all-to-all(bf16[128,2,2048]{2,1,0:T(2,128)(2,1)S(1)} %reshape_squeeze.3), channel_id=1, replica_groups=mesh['rep'=4,'fsdp'=32,'tp'=4] {'rep','fsdp'}, dimensions={0} | all-to-all | bytes 2097152 | tf_op jit(solution)/shard_map/all_to_all | solution.py:14
  83.8 1.0 convert_reduce_fusion
  84.9 0.0 copy-done.1
  84.9 0.0 copy-done.2
  84.9 0.8 fusion.5
  85.7 0.8 copy.33
  86.5 0.0 all-gather.2.cloned.1.call-update
  86.5 20.0 %all-gather.2.cloned.1.call-done = bf16[4,32,2,2048]{3,1,2,0:T(8,128)(2,1)} async-done(((bf16[1,32,2,2048]{3,1,2,0:T(8,128)(2,1)}), bf16[4,32,2,2048]{3,1,2,0:T(8,128)(2,1)}) %all-gather.2.cloned.1.call-update) | async-done | bytes 1048592 | tf_op jit(solution)/shard_map/all_gather | solution.py:23
  106.4 3.3 %copy.34 = bf16[4,32,2,2048]{3,2,0,1:T(2,128)(2,1)} copy(bf16[4,32,2,2048]{3,1,2,0:T(8,128)(2,1)} %all-gather.2.cloned.1.call-done) | data formatting | bytes 2097152 | tf_op jit(solution)/shard_map/all_gather | solution.py:23
  109.7 14.9 %all-to-all-start.1 = ((bf16[4,32,2,2048]{3,2,0,1:T(2,128)(2,1)}), bf16[4,32,2,2048]{3,2,0,1:T(2,128)(2,1)S(1)}, u32[]{:S(2)}, u32[]{:S(2)}) async-start(bf16[4,32,2,2048]{3,2,0,1:T(2,128)(2,1)} %copy.34), calls=%async_computation.1 | async-start | bytes 2097152 | tf_op jit(solution)/shard_map/all_to_all | solution.py:24
  124.6 1.8 fusion.7
  126.4 54.6 %all-to-all-done.1 = bf16[4,32,2,2048]{3,2,0,1:T(2,128)(2,1)S(1)} async-done(((bf16[4,32,2,2048]{3,2,0,1:T(2,128)(2,1)}), bf16[4,32,2,2048]{3,2,0,1:T(2,128)(2,1)S(1)}, u32[]{:S(2)}, u32[]{:S(2)}) %all-to-all-start.1) | async-done | bytes 1048608 | tf_op jit(solution)/shard_map/all_to_all | solution.py:24
  181.0 0.6 copy_convert_fusion
  181.7 1.6 copy.36
  183.3 0.0 copy-start
  183.3 2.5 %reshape.88 = f32[1,256,2048]{2,1,0:T(8,128)} reshape(f32[4,32,2,2048]{3,2,1,0:T(2,128)S(1)} %copy.36) | data formatting | bytes 4194304 | tf_op jit(solution)/shard_map/convert_element_type | solution.py:25
  185.8 0.0 copy-done
  185.8 2.9 %multiply_convert_fusion = bf16[1,256,2048]{2,1,0:T(8,128)(2,1)} fusion(f32[1,256,2048]{2,1,0:T(8,128)} %reshape.88, bf16[1,256,2048]{2,1,0:T(8,128)(2,1)S(1)} %copy-done), kind=kLoop, calls=%fused_computation.1 | loop fusion | flops 2097152 | bytes 4194304 | tf_op jit(solution)/shard_map/convert_element_type | solution.py:26
Async XLA Ops:
  7.2 99.3 %all-gather.2.cloned.1.call-start = ((), (), s32[]{:S(2)}) async-start(), calls=%async_computation.2 | async-start | bytes 1310720 | tf_op jit(solution)/shard_map/all_gather | solution.py:23
  9.0 75.9 %copy-start.1 = (f32[32,1,2,2048]{3,2,1,0:T(2,128)S(1)}, f32[32,1,2,2048]{3,2,1,0:T(2,128)}, u32[]{:S(2)}) copy-start(f32[32,1,2,2048]{3,2,1,0:T(2,128)} %param.4) | copy-start | bytes 1572868
  9.0 75.9 %copy-start.2 = (f32[32,1,2,2048]{3,2,1,0:T(2,128)S(1)}, f32[32,1,2,2048]{3,2,1,0:T(2,128)}, u32[]{:S(2)}) copy-start(f32[32,1,2,2048]{3,2,1,0:T(2,128)} %param.5) | copy-start | bytes 1572868
  109.7 71.3 %all-to-all-start.1 = ((bf16[4,32,2,2048]{3,2,0,1:T(2,128)(2,1)}), bf16[4,32,2,2048]{3,2,0,1:T(2,128)(2,1)S(1)}, u32[]{:S(2)}, u32[]{:S(2)}) async-start(bf16[4,32,2,2048]{3,2,0,1:T(2,128)(2,1)} %copy.34), calls=%async_computation.1 | async-start | bytes 2097152 | tf_op jit(solution)/shard_map/all_to_all | solution.py:24
  183.3 2.5 %copy-start = (bf16[1,256,2048]{2,1,0:T(8,128)(2,1)S(1)}, bf16[1,256,2048]{2,1,0:T(8,128)(2,1)}, u32[]{:S(2)}) copy-start(bf16[1,256,2048]{2,1,0:T(8,128)(2,1)} %param.3) | copy-start | bytes 3145732
Sparse Core Ops, SparseCore 0:
  86.6 19.7 all-gather.1
where the time goes:
time: 196 us
  blocking collectives  74.9 us (38%)
  waiting for transfers between devices  74.6 us (38%)
  starting transfers between devices  15 us (8%)
  between operations  14.1 us (7%)
  local copies, waits for them, and re-layouts  9.96 us (5%)
  other arithmetic  7.05 us (4%)
    all_to_all x1, blocking collectives, on_device(): lax.all_to_all(pieces, ('rep', 'fsdp'), split_axis=0, concat_axis=0, tile...  74.9 us
    all_to_all x1, waiting for transfers between devices, on_device(): lax.all_to_all(copies, 'fsdp', split_axis=1, concat_axis=1, tiled=True)  54.6 us
    all_gather x1, waiting for transfers between devices, on_device(): copies = lax.all_gather(outer_copy[None], 'rep', axis=0, tiled=True)  20 us
    all_to_all x1, starting transfers between devices, on_device(): lax.all_to_all(copies, 'fsdp', split_axis=1, concat_axis=1, tiled=True)  14.9 us
    convert_element_type x2, local copies, waits for them, and re-layouts, on_device(): outer_rows = every_rows.reshape(rows_here, columns).astype(jnp.float32)  4.13 us
  transfers between devices with their start and end apart: 2, of which 2 were waited for; matrix products, arithmetic and copies ran while one was open for 1% of the time, Pallas kernels for 0%

commit v1 on v0

v1 whole, which is shorter than its diff:
```python
import jax
import jax.numpy as jnp
from jax import lax
from jax.sharding import PartitionSpec as P

CORE_SWAP = [(0, 1), (1, 0), (2, 3), (3, 2)]
CHIP_SWAP = [(0, 2), (2, 0), (1, 3), (3, 1)]
F32 = jnp.float32
BF16 = jnp.bfloat16


def on_device(inner_weights, outer_weights, outer_momentum):
    shard = inner_weights[0]
    rows_here, columns = shard.shape
    replicas = lax.axis_size("rep")
    blocks = lax.axis_size("fsdp")
    group = rows_here // (replicas * blocks)
    rep = lax.axis_index("rep")
    chip, core = rep // 2, rep % 2

    parts = shard.reshape(2, 2, rows_here // 4, columns)
    mine = lax.dynamic_index_in_dim(parts, core, 1, keepdims=False)
    other = lax.dynamic_index_in_dim(parts, 1 - core, 1, keepdims=False)
    pair = mine.astype(F32) + lax.ppermute(other, "rep", CORE_SWAP).astype(F32)
    pair_mine = lax.dynamic_index_in_dim(pair, chip, 0, keepdims=False)
    pair_other = lax.dynamic_index_in_dim(pair, 1 - chip, 0, keepdims=False)
    came = lax.ppermute(pair_other.astype(BF16), "rep", CHIP_SWAP)
    total = (pair_mine + came.astype(F32)).astype(BF16)

    inner_total = lax.all_to_all(
        total.reshape(blocks, group, columns), "fsdp", split_axis=0, concat_axis=0, tiled=True
    ).astype(F32)
    outer_here = outer_weights[:, 0]
    pseudo_grad = outer_here - inner_total / replicas
    new_momentum = 0.9 * outer_momentum[:, 0] + pseudo_grad
    new_outer = outer_here - 0.7 * (pseudo_grad + 0.9 * new_momentum)
    outer_copy = new_outer.astype(BF16)

    back = lax.all_to_all(outer_copy, "fsdp", split_axis=0, concat_axis=0, tiled=True)
    back = back.reshape(rows_here // 4, columns)
    across = lax.ppermute(back, "rep", CHIP_SWAP)
    two = jnp.where(chip == 0, jnp.stack([back, across]), jnp.stack([across, back]))
    beside = lax.ppermute(two, "rep", CORE_SWAP)
    rows = jnp.where(core == 0, jnp.stack([two, beside], 1), jnp.stack([beside, two], 1))
    outer_rows = rows.reshape(rows_here, columns).astype(F32)
    mixed = (0.5 * shard.astype(F32) + 0.5 * outer_rows).astype(BF16)
    return (mixed[None], new_outer[:, None], new_momentum[:, None])


def solution(mesh):
    in_specs = (
        P("rep", "fsdp", "tp"),
        P(None, ("rep", "fsdp"), None, "tp"),
        P(None, ("rep", "fsdp"), None, "tp"),
    )
    out_specs = (
        P("rep", "fsdp", "tp"),
        P(None, ("rep", "fsdp"), None, "tp"),
        P(None, ("rep", "fsdp"), None, "tp"),
    )
    return jax.shard_map(
        on_device, mesh=mesh, in_specs=in_specs, out_specs=out_specs, check_vma=False
    )
```

time: 196 us -> 103 us (0.53)
  the two profiles are of different devices: /device:TPU:32 before, /device:TPU:1 now
where the time goes in v1:
time: 103 us; the launch traced here: 102 us
  blocking collectives  58.3 us (57%)
  starting transfers between devices  20.7 us (20%)
  waiting for transfers between devices  15 us (15%)
  other arithmetic  4.72 us (5%)
  local copies, waits for them, and re-layouts  2.83 us (3%)
    all_to_all x1, blocking collectives, on_device(): lax.all_to_all(total.reshape(blocks, group, columns), 'fsdp', split_axis=...  32.8 us
    all_to_all x1, blocking collectives, on_device(): lax.all_to_all(outer_copy, 'fsdp', split_axis=0, concat_axis=0, tiled=True)  25.4 us
    ppermute x1, starting transfers between devices, on_device(): pair = mine.astype(F32) + lax.ppermute(other, 'rep', CORE_SWAP).astype(F32)  8.79 us
    ppermute x1, starting transfers between devices, on_device(): beside = lax.ppermute(two, 'rep', CORE_SWAP)  7.79 us
    ppermute x1, waiting for transfers between devices, on_device(): came = lax.ppermute(pair_other.astype(BF16), 'rep', CHIP_SWAP)  7.48 us
    ppermute x1, waiting for transfers between devices, on_device(): across = lax.ppermute(back, 'rep', CHIP_SWAP)  4.77 us
    ppermute x1, starting transfers between devices, on_device(): across = lax.ppermute(back, 'rep', CHIP_SWAP)  2.22 us
  transfers between devices with their start and end apart: 4, of which 4 were waited for; matrix products, arithmetic and copies ran while one was open for 0% of the time, Pallas kernels for 0%

profile of v1, /device:TPU:1, one launch (start us, length us, event | category | flops | bytes accessed | tf_op | source)
XLA Modules:
  0.0 102.4 jit_solution(2214304566658816583)
XLA Ops:
  0.6 1.1 %dynamic-slice_bitcast_fusion = bf16[2,64,2048]{2,1,0:T(8,128)(2,1)S(1)} fusion(bf16[2,2,64,2048]{3,2,1,0:T(8,128)(2,1)} %bitcast.51, s32[]{:T(128)S(6)} %select_n.66), kind=kLoop, calls=%fused_computation.13 | loop fusion | bytes 1048580 | tf_op jit(solution)/shard_map/jit(dynamic_index_in_dim)/squeeze | solution.py:23
  1.7 8.8 %collective-permute-start = (bf16[2,64,2048]{2,1,0:T(8,128)(2,1)S(1)}, bf16[2,64,2048]{2,1,0:T(8,128)(2,1)S(1)}, u32[]{:S(2)}, u32[]{:S(2)}) collective-permute-start(bf16[2,64,2048]{2,1,0:T(8,128)(2,1)S(1)} %dynamic-slice_bitcast_fusion), channel_id=1, source_target_pairs={{0,128},{128,0},{256,384},{384,256},{1,129},{129,1},{257,385},{385... | collective-permute-start | bytes 1572872 | tf_op jit(solution)/shard_map/ppermute | solution.py:24
  10.6 0.0 copy-start.1
  10.6 0.0 copy-start.2
  10.6 1.5 %collective-permute-done = bf16[2,64,2048]{2,1,0:T(8,128)(2,1)S(1)} collective-permute-done((bf16[2,64,2048]{2,1,0:T(8,128)(2,1)S(1)}, bf16[2,64,2048]{2,1,0:T(8,128)(2,1)S(1)}, u32[]{:S(2)}, u32[]{:S(2)}) %collective-permute-start) | collective-permute-done | bytes 524320 | tf_op jit(solution)/shard_map/ppermute | solution.py:24
  12.0 1.2 %convert_add_fusion = f32[2,64,2048]{2,1,0:T(8,128)S(1)} fusion(bf16[2,64,2048]{2,1,0:T(8,128)(2,1)S(1)} %collective-permute-done, bf16[2,2,64,2048]{3,2,1,0:T(8,128)(2,1)} %bitcast.52, s32[]{:T(128)S(6)} %select_n.65), kind=kLoop, calls=%fused_computation.3 | loop fusion | flops 786432 | bytes 2097156 | tf_op jit(solution)/shard_map/add | solution.py:24
  13.3 1.9 %collective-permute-start.1 = (bf16[64,2048]{1,0:T(8,128)(2,1)S(1)}, bf16[64,2048]{1,0:T(8,128)(2,1)S(1)}, u32[]{:S(2)}, u32[]{:S(2)}) collective-permute-start(bf16[64,2048]{1,0:T(8,128)(2,1)S(1)} %fusion.2), channel_id=1, source_target_pairs={{0,256},{256,0},{128,384},{384,128},{1,257},{257,1},{129,385},{385... | collective-permute-start | bytes 786440 | tf_op jit(solution)/shard_map/ppermute | solution.py:27
  15.2 7.5 %collective-permute-done.1 = bf16[64,2048]{1,0:T(8,128)(2,1)S(1)} collective-permute-done((bf16[64,2048]{1,0:T(8,128)(2,1)S(1)}, bf16[64,2048]{1,0:T(8,128)(2,1)S(1)}, u32[]{:S(2)}, u32[]{:S(2)}) %collective-permute-start.1) | collective-permute-done | bytes 262176 | tf_op jit(solution)/shard_map/ppermute | solution.py:27
  22.7 0.2 reshape.103
  22.9 32.8 %all_to_all.10 = bf16[32,2,2048]{2,1,0:T(2,128)(2,1)S(1)} all-to-all(bf16[32,2,2048]{2,1,0:T(2,128)(2,1)S(1)} %reshape.103), channel_id=1, replica_groups=mesh['rep'=4,'fsdp'=32,'tp'=4] {'fsdp'}, dimensions={0} | all-to-all | bytes 524288 | tf_op jit(solution)/shard_map/all_to_all | solution.py:30
  55.7 0.0 copy-done.1
  55.7 0.0 copy-done.2
  55.7 1.9 %fusion.4 = (bf16[32,2,2048]{2,1,0:T(2,128)(2,1)S(1)}, f32[32,2,2048]{2,1,0:T(2,128)}, f32[32,1,2,2048]{3,2,1,0:T(2,128)}) fusion(f32[32,1,2,2048]{3,2,1,0:T(2,128)S(1)} %copy-done.1, bf16[32,2,2048]{2,1,0:T(2,128)(2,1)S(1)} %all_to_all.10, f32[32,1,2,2048]{3,2,1,0:T(2,128)S(1)} %copy-done.2), kind=kLoop, calls=%fused_computation.16 | loop fusion | flops 1310720 | bytes 2621440 | tf_op jit(solution)/shard_map/convert_element_type | solution.py:37
  57.6 25.4 %all_to_all.11 = bf16[32,2,2048]{2,1,0:T(2,128)(2,1)S(1)} all-to-all(bf16[32,2,2048]{2,1,0:T(2,128)(2,1)S(1)} %get-tuple-element.3), channel_id=1, replica_groups=mesh['rep'=4,'fsdp'=32,'tp'=4] {'fsdp'}, dimensions={0} | all-to-all | bytes 524288 | tf_op jit(solution)/shard_map/all_to_all | solution.py:39
  83.0 0.1 reshape.104
  83.1 2.2 %collective-permute-start.2 = (bf16[64,2048]{1,0:T(8,128)(2,1)S(1)}, bf16[64,2048]{1,0:T(8,128)(2,1)S(1)}, u32[]{:S(2)}, u32[]{:S(2)}) collective-permute-start(bf16[64,2048]{1,0:T(8,128)(2,1)S(1)} %reshape.104), channel_id=1, source_target_pairs={{0,256},{256,0},{128,384},{384,128},{1,257},{257,1},{129,385},{385... | collective-permute-start | bytes 786440 | tf_op jit(solution)/shard_map/ppermute | solution.py:41
  85.4 0.1 stack_reshape.4
  85.5 4.8 %collective-permute-done.2 = bf16[64,2048]{1,0:T(8,128)(2,1)S(1)} collective-permute-done((bf16[64,2048]{1,0:T(8,128)(2,1)S(1)}, bf16[64,2048]{1,0:T(8,128)(2,1)S(1)}, u32[]{:S(2)}, u32[]{:S(2)}) %collective-permute-start.2) | collective-permute-done | bytes 262176 | tf_op jit(solution)/shard_map/ppermute | solution.py:41
  90.2 0.1 maximum_select_fusion.2
  90.3 7.8 %collective-permute-start.3 = (bf16[2,64,2048]{2,1,0:T(8,128)(2,1)S(1)}, bf16[2,64,2048]{2,1,0:T(8,128)(2,1)S(1)}, u32[]{:S(2)}, u32[]{:S(2)}) collective-permute-start(bf16[2,64,2048]{2,1,0:T(8,128)(2,1)S(1)} %maximum_select_fusion.2), channel_id=1, source_target_pairs={{0,128},{128,0},{256,384},{384,256},{1,129},{129,1},{257,385},{385... | collective-permute-start | bytes 1572872 | tf_op jit(solution)/shard_map/ppermute | solution.py:43
  98.1 0.1 stack.30
  98.2 0.1 maximum_select_fusion.1
  98.3 1.3 %collective-permute-done.3 = bf16[2,64,2048]{2,1,0:T(8,128)(2,1)S(1)} collective-permute-done((bf16[2,64,2048]{2,1,0:T(8,128)(2,1)S(1)}, bf16[2,64,2048]{2,1,0:T(8,128)(2,1)S(1)}, u32[]{:S(2)}, u32[]{:S(2)}) %collective-permute-start.3) | collective-permute-done | bytes 524320 | tf_op jit(solution)/shard_map/ppermute | solution.py:43
  99.6 0.2 fusion
  99.9 0.0 copy-start
  99.9 0.2 copy.10
  100.1 1.0 copy-done
  101.1 1.3 %multiply_convert_fusion = bf16[1,256,2048]{2,1,0:T(8,128)(2,1)} fusion(f32[1,256,2048]{2,1,0:T(8,128)S(1)} %bitcast.50, bf16[1,256,2048]{2,1,0:T(8,128)(2,1)S(1)} %copy-done), kind=kLoop, calls=%fused_computation | loop fusion | flops 2097152 | bytes 4194304 | tf_op jit(solution)/shard_map/convert_element_type | solution.py:46
  (2 shorter events, 0.1 us)
Async XLA Ops:
  1.7 10.3 %collective-permute-start = (bf16[2,64,2048]{2,1,0:T(8,128)(2,1)S(1)}, bf16[2,64,2048]{2,1,0:T(8,128)(2,1)S(1)}, u32[]{:S(2)}, u32[]{:S(2)}) collective-permute-start(bf16[2,64,2048]{2,1,0:T(8,128)(2,1)S(1)} %dynamic-slice_bitcast_fusion), channel_id=1, source_target_pairs={{0,128},{128,0},{256,384},{384,256},{1,129},{129,1},{257,385},{385... | collective-permute-start | bytes 1572872 | tf_op jit(solution)/shard_map/ppermute | solution.py:24
  10.6 45.2 %copy-start.1 = (f32[32,1,2,2048]{3,2,1,0:T(2,128)S(1)}, f32[32,1,2,2048]{3,2,1,0:T(2,128)}, u32[]{:S(2)}) copy-start(f32[32,1,2,2048]{3,2,1,0:T(2,128)} %param.5) | copy-start | bytes 1572868
  10.6 45.2 %copy-start.2 = (f32[32,1,2,2048]{3,2,1,0:T(2,128)S(1)}, f32[32,1,2,2048]{3,2,1,0:T(2,128)}, u32[]{:S(2)}) copy-start(f32[32,1,2,2048]{3,2,1,0:T(2,128)} %param.4) | copy-start | bytes 1572868
  13.3 9.4 %collective-permute-start.1 = (bf16[64,2048]{1,0:T(8,128)(2,1)S(1)}, bf16[64,2048]{1,0:T(8,128)(2,1)S(1)}, u32[]{:S(2)}, u32[]{:S(2)}) collective-permute-start(bf16[64,2048]{1,0:T(8,128)(2,1)S(1)} %fusion.2), channel_id=1, source_target_pairs={{0,256},{256,0},{128,384},{384,128},{1,257},{257,1},{129,385},{385... | collective-permute-start | bytes 786440 | tf_op jit(solution)/shard_map/ppermute | solution.py:27
  83.1 7.1 %collective-permute-start.2 = (bf16[64,2048]{1,0:T(8,128)(2,1)S(1)}, bf16[64,2048]{1,0:T(8,128)(2,1)S(1)}, u32[]{:S(2)}, u32[]{:S(2)}) collective-permute-start(bf16[64,2048]{1,0:T(8,128)(2,1)S(1)} %reshape.104), channel_id=1, source_target_pairs={{0,256},{256,0},{128,384},{384,128},{1,257},{257,1},{129,385},{385... | collective-permute-start | bytes 786440 | tf_op jit(solution)/shard_map/ppermute | solution.py:41
  90.3 9.3 %collective-permute-start.3 = (bf16[2,64,2048]{2,1,0:T(8,128)(2,1)S(1)}, bf16[2,64,2048]{2,1,0:T(8,128)(2,1)S(1)}, u32[]{:S(2)}, u32[]{:S(2)}) collective-permute-start(bf16[2,64,2048]{2,1,0:T(8,128)(2,1)S(1)} %maximum_select_fusion.2), channel_id=1, source_target_pairs={{0,128},{128,0},{256,384},{384,256},{1,129},{129,1},{257,385},{385... | collective-permute-start | bytes 1572872 | tf_op jit(solution)/shard_map/ppermute | solution.py:43
  99.9 1.2 %copy-start = (bf16[1,256,2048]{2,1,0:T(8,128)(2,1)S(1)}, bf16[1,256,2048]{2,1,0:T(8,128)(2,1)}, u32[]{:S(2)}) copy-start(bf16[1,256,2048]{2,1,0:T(8,128)(2,1)} %param.3) | copy-start | bytes 3145732

commit v2 on v1

--- a/solution.py
+++ b/solution.py
@@ -17,6 +17,12 @@
     group = rows_here // (replicas * blocks)
     rep = lax.axis_index("rep")
     chip, core = rep // 2, rep % 2
+    outer_here = outer_weights[:, 0]
+    momentum_here = outer_momentum[:, 0]
+
+    state_part = (-0.33 * outer_here - 0.567 * momentum_here).astype(BF16)
+    state_rows = lax.all_to_all(state_part, "fsdp", split_axis=0, concat_axis=0, tiled=True)
+    state_rows = state_rows.reshape(rows_here // 4, columns)
 
     parts = shard.reshape(2, 2, rows_here // 4, columns)
     mine = lax.dynamic_index_in_dim(parts, core, 1, keepdims=False)
@@ -25,25 +31,24 @@
     pair_mine = lax.dynamic_index_in_dim(pair, chip, 0, keepdims=False)
     pair_other = lax.dynamic_index_in_dim(pair, 1 - chip, 0, keepdims=False)
     came = lax.ppermute(pair_other.astype(BF16), "rep", CHIP_SWAP)
-    total = (pair_mine + came.astype(F32)).astype(BF16)
+    total = pair_mine + came.astype(F32)
 
     inner_total = lax.all_to_all(
-        total.reshape(blocks, group, columns), "fsdp", split_axis=0, concat_axis=0, tiled=True
+        total.astype(BF16).reshape(blocks, group, columns),
+        "fsdp", split_axis=0, concat_axis=0, tiled=True,
     ).astype(F32)
-    outer_here = outer_weights[:, 0]
-    pseudo_grad = outer_here - inner_total / replicas
-    new_momentum = 0.9 * outer_momentum[:, 0] + pseudo_grad
-    new_outer = outer_here - 0.7 * (pseudo_grad + 0.9 * new_momentum)
-    outer_copy = new_outer.astype(BF16)
 
-    back = lax.all_to_all(outer_copy, "fsdp", split_axis=0, concat_axis=0, tiled=True)
-    back = back.reshape(rows_here // 4, columns)
-    across = lax.ppermute(back, "rep", CHIP_SWAP)
-    two = jnp.where(chip == 0, jnp.stack([back, across]), jnp.stack([across, back]))
+    copy = (state_rows.astype(F32) + 0.3325 * total).astype(BF16)
+    across = lax.ppermute(copy, "rep", CHIP_SWAP)
+    two = jnp.where(chip == 0, jnp.stack([copy, across]), jnp.stack([across, copy]))
     beside = lax.ppermute(two, "rep", CORE_SWAP)
     rows = jnp.where(core == 0, jnp.stack([two, beside], 1), jnp.stack([beside, two], 1))
     outer_rows = rows.reshape(rows_here, columns).astype(F32)
     mixed = (0.5 * shard.astype(F32) + 0.5 * outer_rows).astype(BF16)
+
+    pseudo_grad = outer_here - inner_total / replicas
+    new_momentum = 0.9 * momentum_here + pseudo_grad
+    new_outer = outer_here - 0.7 * (pseudo_grad + 0.9 * new_momentum)
     return (mixed[None], new_outer[:, None], new_momentum[:, None])
 
 

time: 103 us -> 91.1 us (0.88)
  blocking collectives: 58.3 us -> 0 us
  waiting for transfers between devices: 15 us -> 43.9 us
  starting transfers between devices: 20.7 us -> 35.3 us
  other arithmetic: 4.72 us -> 7.29 us
    all_to_all x2 -> x0, blocking collectives: 58.3 us -> none  [the longest x1 32.8 us: on_device(): lax.all_to_all(total.reshape(blocks, group, columns), 'fsdp', split_axis=...]
    all_to_all x0 -> x2, waiting for transfers between devices: none -> 39.1 us  [the longest x1 19.8 us: on_device(): lax.all_to_all(state_part, 'fsdp', split_axis=0, concat_axis=0, tiled=True)]
    all_to_all x0 -> x2, starting transfers between devices: none -> 16.7 us  [the longest x1 12.3 us: on_device(): lax.all_to_all(state_part, 'fsdp', split_axis=0, concat_axis=0, tiled=True)]
    ppermute x1, waiting for transfers between devices: 7.48 us -> 0.01 us  [on_device(): came = lax.ppermute(pair_other.astype(BF16), 'rep', CHIP_SWAP)]
    ppermute x1, starting transfers between devices: 7.79 us -> 5.44 us  [on_device(): beside = lax.ppermute(two, 'rep', CORE_SWAP)]
    broadcast_in_dim x0 -> x1, other arithmetic: none -> 1.78 us  [on_device(): return (mixed[None], new_outer[:, None], new_momentum[:, None])]
    ppermute x1, waiting for transfers between devices: 1.46 us -> 0.01 us  [on_device(): pair = mine.astype(F32) + lax.ppermute(other, 'rep', CORE_SWAP).astype(F32)]
    ppermute x1, waiting for transfers between devices: 1.32 us -> 0.01 us  [on_device(): beside = lax.ppermute(two, 'rep', CORE_SWAP)]
  transfers between devices with their start and end apart: 4 -> 6, of which waited for: 4 -> 3; matrix products, arithmetic and copies ran while one was open for 0% -> 7% of each run, Pallas kernels for 0% -> 0%
where the time goes in v2:
time: 91.1 us; the launch traced here: 89.8 us
  waiting for transfers between devices  43.9 us (48%)
  starting transfers between devices  35.3 us (39%)
  other arithmetic  7.29 us (8%)
  local copies, waits for them, and re-layouts  2.4 us (3%)
    all_to_all x1, waiting for transfers between devices, on_device(): lax.all_to_all(state_part, 'fsdp', split_axis=0, concat_axis=0, tiled=True)  19.8 us
    all_to_all x1, waiting for transfers between devices, on_device(): lax.all_to_all(total.astype(BF16).reshape(blocks, group, columns), 'fsdp'...  19.2 us
    all_to_all x1, starting transfers between devices, on_device(): lax.all_to_all(state_part, 'fsdp', split_axis=0, concat_axis=0, tiled=True)  12.3 us
    ppermute x1, starting transfers between devices, on_device(): pair = mine.astype(F32) + lax.ppermute(other, 'rep', CORE_SWAP).astype(F32)  8.79 us
    ppermute x1, starting transfers between devices, on_device(): beside = lax.ppermute(two, 'rep', CORE_SWAP)  5.44 us
    ppermute x1, waiting for transfers between devices, on_device(): across = lax.ppermute(copy, 'rep', CHIP_SWAP)  4.88 us
    all_to_all x1, starting transfers between devices, on_device(): lax.all_to_all(total.astype(BF16).reshape(blocks, group, columns), 'fsdp'...  4.39 us
    convert_element_type x1, other arithmetic, on_device(): state_part = (-0.33 * outer_here - 0.567 * momentum_here).astype(BF16)  2.41 us
  transfers between devices with their start and end apart: 6, of which 3 were waited for; matrix products, arithmetic and copies ran while one was open for 7% of the time, Pallas kernels for 0%

profile of v2, /device:TPU:1, one launch (start us, length us, event | category | flops | bytes accessed | tf_op | source)
XLA Modules:
  0.0 89.8 jit_solution(9315162635634226577)
XLA Ops:
  0.6 0.0 copy-start
  0.7 1.2 %dynamic-slice_bitcast_fusion = bf16[2,64,2048]{2,1,0:T(8,128)(2,1)S(1)} fusion(bf16[2,2,64,2048]{3,2,1,0:T(8,128)(2,1)} %bitcast.64, s32[]{:T(128)S(6)} %select_n.66), kind=kLoop, calls=%fused_computation.18 | loop fusion | bytes 1048580 | tf_op jit(solution)/shard_map/jit(dynamic_index_in_dim)/squeeze | solution.py:29
  1.8 8.8 %collective-permute-start = (bf16[2,64,2048]{2,1,0:T(8,128)(2,1)S(1)}, bf16[2,64,2048]{2,1,0:T(8,128)(2,1)S(1)}, u32[]{:S(2)}, u32[]{:S(2)}) collective-permute-start(bf16[2,64,2048]{2,1,0:T(8,128)(2,1)S(1)} %dynamic-slice_bitcast_fusion), channel_id=1, source_target_pairs={{0,128},{128,0},{256,384},{384,256},{1,129},{129,1},{257,385},{385... | collective-permute-start | bytes 1572872 | tf_op jit(solution)/shard_map/ppermute | solution.py:30
  10.6 2.4 %fusion.1 = bf16[32,2,2048]{2,1,0:T(2,128)(2,1)} fusion(f32[32,1,2,2048]{3,2,1,0:T(2,128)} %param.5, f32[32,1,2,2048]{3,2,1,0:T(2,128)} %param.4), kind=kLoop, calls=%fused_computation.9 | loop fusion | flops 524288 | bytes 1310720 | tf_op jit(solution)/shard_map/convert_element_type | solution.py:23
  13.0 12.3 %all-to-all-start = ((bf16[32,2,2048]{2,1,0:T(2,128)(2,1)}), bf16[32,2,2048]{2,1,0:T(2,128)(2,1)S(1)}, u32[]{:S(2)}, u32[]{:S(2)}) async-start(bf16[32,2,2048]{2,1,0:T(2,128)(2,1)} %fusion.1), calls=%async_computation | async-start | bytes 524288 | tf_op jit(solution)/shard_map/all_to_all | solution.py:24
  25.4 0.0 collective-permute-done
  25.4 0.0 copy-done
  25.4 0.1 convert_add_fusion
  25.6 2.2 %collective-permute-start.1 = (bf16[64,2048]{1,0:T(8,128)(2,1)S(1)}, bf16[64,2048]{1,0:T(8,128)(2,1)S(1)}, u32[]{:S(2)}, u32[]{:S(2)}) collective-permute-start(bf16[64,2048]{1,0:T(8,128)(2,1)S(1)} %fusion.4), channel_id=1, source_target_pairs={{0,256},{256,0},{128,384},{384,128},{1,257},{257,1},{129,385},{385... | collective-permute-start | bytes 786440 | tf_op jit(solution)/shard_map/ppermute | solution.py:33
  27.8 19.8 %all-to-all-done = bf16[32,2,2048]{2,1,0:T(2,128)(2,1)S(1)} async-done(((bf16[32,2,2048]{2,1,0:T(2,128)(2,1)}), bf16[32,2,2048]{2,1,0:T(2,128)(2,1)S(1)}, u32[]{:S(2)}, u32[]{:S(2)}) %all-to-all-start) | async-done | bytes 262176 | tf_op jit(solution)/shard_map/all_to_all | solution.py:24
  47.6 0.1 reshape.106
  47.7 0.0 collective-permute-done.1
  47.7 0.1 fusion.3
  47.8 2.2 %collective-permute-start.2 = (bf16[64,2048]{1,0:T(8,128)(2,1)S(1)}, bf16[64,2048]{1,0:T(8,128)(2,1)S(1)}, u32[]{:S(2)}, u32[]{:S(2)}) collective-permute-start(bf16[64,2048]{1,0:T(8,128)(2,1)S(1)} %get-tuple-element.6), channel_id=1, source_target_pairs={{0,256},{256,0},{128,384},{384,128},{1,257},{257,1},{129,385},{385... | collective-permute-start | bytes 786440 | tf_op jit(solution)/shard_map/ppermute | solution.py:42
  50.1 4.9 %collective-permute-done.2 = bf16[64,2048]{1,0:T(8,128)(2,1)S(1)} collective-permute-done((bf16[64,2048]{1,0:T(8,128)(2,1)S(1)}, bf16[64,2048]{1,0:T(8,128)(2,1)S(1)}, u32[]{:S(2)}, u32[]{:S(2)}) %collective-permute-start.2) | collective-permute-done | bytes 262176 | tf_op jit(solution)/shard_map/ppermute | solution.py:42
  54.9 0.1 maximum_select_fusion.2
  55.0 5.4 %collective-permute-start.3 = (bf16[2,64,2048]{2,1,0:T(8,128)(2,1)S(1)}, bf16[2,64,2048]{2,1,0:T(8,128)(2,1)}, u32[]{:S(2)}, u32[]{:S(2)}) collective-permute-start(bf16[2,64,2048]{2,1,0:T(8,128)(2,1)S(1)} %maximum_select_fusion.2), channel_id=1, source_target_pairs={{0,128},{128,0},{256,384},{384,256},{1,129},{129,1},{257,385},{385... | collective-permute-start | bytes 1572872 | tf_op jit(solution)/shard_map/ppermute | solution.py:44
  60.5 0.9 reshape.105
  61.4 4.4 %all-to-all-start.1 = ((bf16[32,2,2048]{2,1,0:T(2,128)(2,1)}), bf16[32,2,2048]{2,1,0:T(2,128)(2,1)S(1)}, u32[]{:S(2)}, u32[]{:S(2)}) async-start(bf16[32,2,2048]{2,1,0:T(2,128)(2,1)} %reshape.105), calls=%async_computation.1 | async-start | bytes 524288 | tf_op jit(solution)/shard_map/all_to_all | solution.py:36
  65.8 0.1 maximum_select_fusion.1
  65.8 0.0 collective-permute-done.3
  65.9 1.4 %fusion = f32[2,2,64,2048]{3,2,0,1:T(8,128)S(1)} fusion(bf16[2,1,64,2048]{3,2,0,1:T(8,128)(2,1)} %bitcast.12, bf16[2,1,64,2048]{3,2,0,1:T(8,128)(2,1)S(1)} %maximum_select_fusion.1, pred[]{:T(512)S(6)} %eq.8), kind=kLoop, calls=%fused_computation.2 | loop fusion | flops 2097152 | bytes 3145729 | tf_op jit(solution)/shard_map/convert_element_type | solution.py:46
  67.3 0.2 copy.8
  67.5 0.0 copy-start.1
  67.5 0.0 copy-start.2
  67.5 1.3 %multiply_convert_fusion = bf16[1,256,2048]{2,1,0:T(8,128)(2,1)} fusion(f32[1,256,2048]{2,1,0:T(8,128)S(1)} %bitcast.63, bf16[1,256,2048]{2,1,0:T(8,128)(2,1)S(1)} %copy-done), kind=kLoop, calls=%fused_computation | loop fusion | flops 2097152 | bytes 4194304 | tf_op jit(solution)/shard_map/convert_element_type | solution.py:47
  68.8 19.2 %all-to-all-done.1 = bf16[32,2,2048]{2,1,0:T(2,128)(2,1)S(1)} async-done(((bf16[32,2,2048]{2,1,0:T(2,128)(2,1)}), bf16[32,2,2048]{2,1,0:T(2,128)(2,1)S(1)}, u32[]{:S(2)}, u32[]{:S(2)}) %all-to-all-start.1) | async-done | bytes 262176 | tf_op jit(solution)/shard_map/all_to_all | solution.py:36
  88.1 0.0 copy-done.1
  88.1 0.0 copy-done.2
  88.1 1.8 %fusion.5 = (f32[32,1,2,2048]{3,2,1,0:T(2,128)}, f32[32,1,2,2048]{3,2,1,0:T(2,128)}) fusion(bf16[32,2,2048]{2,1,0:T(2,128)(2,1)S(1)} %all-to-all-done.1, f32[32,1,2,2048]{3,2,1,0:T(2,128)S(1)} %copy-done.2, f32[32,1,2,2048]{3,2,1,0:T(2,128)S(1)} %copy-done.1), kind=kLoop, calls=%fused_computation.21 | loop fusion | flops 1179648 | bytes 2359296 | tf_op jit(solution)/shard_map/broadcast_in_dim | solution.py:52
  (1 shorter events, 0.0 us)
Async XLA Ops:
  0.6 24.7 %copy-start = (bf16[1,256,2048]{2,1,0:T(8,128)(2,1)S(1)}, bf16[1,256,2048]{2,1,0:T(8,128)(2,1)}, u32[]{:S(2)}) copy-start(bf16[1,256,2048]{2,1,0:T(8,128)(2,1)} %param.3) | copy-start | bytes 3145732
  1.8 23.5 %collective-permute-start = (bf16[2,64,2048]{2,1,0:T(8,128)(2,1)S(1)}, bf16[2,64,2048]{2,1,0:T(8,128)(2,1)S(1)}, u32[]{:S(2)}, u32[]{:S(2)}) collective-permute-start(bf16[2,64,2048]{2,1,0:T(8,128)(2,1)S(1)} %dynamic-slice_bitcast_fusion), channel_id=1, source_target_pairs={{0,128},{128,0},{256,384},{384,256},{1,129},{129,1},{257,385},{385... | collective-permute-start | bytes 1572872 | tf_op jit(solution)/shard_map/ppermute | solution.py:30
  13.0 34.6 %all-to-all-start = ((bf16[32,2,2048]{2,1,0:T(2,128)(2,1)}), bf16[32,2,2048]{2,1,0:T(2,128)(2,1)S(1)}, u32[]{:S(2)}, u32[]{:S(2)}) async-start(bf16[32,2,2048]{2,1,0:T(2,128)(2,1)} %fusion.1), calls=%async_computation | async-start | bytes 524288 | tf_op jit(solution)/shard_map/all_to_all | solution.py:24
  25.6 22.1 %collective-permute-start.1 = (bf16[64,2048]{1,0:T(8,128)(2,1)S(1)}, bf16[64,2048]{1,0:T(8,128)(2,1)S(1)}, u32[]{:S(2)}, u32[]{:S(2)}) collective-permute-start(bf16[64,2048]{1,0:T(8,128)(2,1)S(1)} %fusion.4), channel_id=1, source_target_pairs={{0,256},{256,0},{128,384},{384,128},{1,257},{257,1},{129,385},{385... | collective-permute-start | bytes 786440 | tf_op jit(solution)/shard_map/ppermute | solution.py:33
  47.8 7.1 %collective-permute-start.2 = (bf16[64,2048]{1,0:T(8,128)(2,1)S(1)}, bf16[64,2048]{1,0:T(8,128)(2,1)S(1)}, u32[]{:S(2)}, u32[]{:S(2)}) collective-permute-start(bf16[64,2048]{1,0:T(8,128)(2,1)S(1)} %get-tuple-element.6), channel_id=1, source_target_pairs={{0,256},{256,0},{128,384},{384,128},{1,257},{257,1},{129,385},{385... | collective-permute-start | bytes 786440 | tf_op jit(solution)/shard_map/ppermute | solution.py:42
  55.0 10.8 %collective-permute-start.3 = (bf16[2,64,2048]{2,1,0:T(8,128)(2,1)S(1)}, bf16[2,64,2048]{2,1,0:T(8,128)(2,1)}, u32[]{:S(2)}, u32[]{:S(2)}) collective-permute-start(bf16[2,64,2048]{2,1,0:T(8,128)(2,1)S(1)} %maximum_select_fusion.2), channel_id=1, source_target_pairs={{0,128},{128,0},{256,384},{384,256},{1,129},{129,1},{257,385},{385... | collective-permute-start | bytes 1572872 | tf_op jit(solution)/shard_map/ppermute | solution.py:44
  61.4 26.7 %all-to-all-start.1 = ((bf16[32,2,2048]{2,1,0:T(2,128)(2,1)}), bf16[32,2,2048]{2,1,0:T(2,128)(2,1)S(1)}, u32[]{:S(2)}, u32[]{:S(2)}) async-start(bf16[32,2,2048]{2,1,0:T(2,128)(2,1)} %reshape.105), calls=%async_computation.1 | async-start | bytes 524288 | tf_op jit(solution)/shard_map/all_to_all | solution.py:36
  67.5 20.6 %copy-start.1 = (f32[32,1,2,2048]{3,2,1,0:T(2,128)S(1)}, f32[32,1,2,2048]{3,2,1,0:T(2,128)}, u32[]{:S(2)}) copy-start(f32[32,1,2,2048]{3,2,1,0:T(2,128)} %param.5) | copy-start | bytes 1572868
  67.5 20.6 %copy-start.2 = (f32[32,1,2,2048]{3,2,1,0:T(2,128)S(1)}, f32[32,1,2,2048]{3,2,1,0:T(2,128)}, u32[]{:S(2)}) copy-start(f32[32,1,2,2048]{3,2,1,0:T(2,128)} %param.4) | copy-start | bytes 1572868

commit v3 on v2

v3 whole, which is shorter than its diff:
```python
import jax
import jax.numpy as jnp
from jax import lax
from jax.experimental import pallas as pl
from jax.experimental.pallas import tpu as pltpu
from jax.sharding import PartitionSpec as P

F32 = jnp.float32
BF16 = jnp.bfloat16
VMEM = pl.BlockSpec(memory_space=pltpu.VMEM)
PARAMS = pltpu.CompilerParams(vmem_limit_bytes=32 * 1024 * 1024)


def cost(nbytes):
    return pl.CostEstimate(flops=0, bytes_accessed=nbytes, transcendentals=0)


def mix_kernel(rep_ref, shard_ref, *refs):
    *copy_refs, out_ref = refs
    rep = rep_ref[0]
    quarter = copy_refs[0].shape[0]
    for i, copy_ref in enumerate(copy_refs):
        rows = pl.ds(pl.multiple_of((rep ^ i) * quarter, quarter), quarter)
        value = 0.5 * shard_ref[rows, :].astype(F32) + 0.5 * copy_ref[...].astype(F32)
        out_ref[rows, :] = value.astype(BF16)


def mix(rep, shard, copies):
    return pl.pallas_call(
        mix_kernel,
        in_specs=[pl.BlockSpec(memory_space=pltpu.SMEM)] + [VMEM] * (1 + len(copies)),
        out_specs=VMEM,
        out_shape=jax.ShapeDtypeStruct(shard.shape, BF16),
        cost_estimate=cost(3 << 20),
        compiler_params=PARAMS,
    )(rep.reshape(1), shard, *copies)


def on_device(inner_weights, outer_weights, outer_momentum):
    shard = inner_weights[0]
    rows_here, columns = shard.shape
    replicas = lax.axis_size("rep")
    blocks = lax.axis_size("fsdp")
    quarter = rows_here // replicas
    group = quarter // blocks
    rep = lax.axis_index("rep")
    chip, core = rep // 2, rep % 2
    outer_here = outer_weights[:, 0]
    momentum_here = outer_momentum[:, 0]

    def exchange(value):
        return lax.all_to_all(value, "fsdp", split_axis=0, concat_axis=0, tiled=True)

    def swap(value, i):
        return lax.ppermute(value, "rep", [(r, r ^ i) for r in range(replicas)])

    state_part = (-0.33 * outer_here - 0.567 * momentum_here).astype(BF16)
    parts = shard.reshape(2, 2, quarter, columns)
    parts, state_part = lax.optimization_barrier((parts, state_part))
    state_rows = exchange(state_part).reshape(quarter, columns)

    other = lax.dynamic_index_in_dim(parts, 1 - core, 1, keepdims=False)
    mine = lax.dynamic_index_in_dim(parts, core, 1, keepdims=False)
    pair = mine.astype(F32) + swap(other, 1).astype(F32)
    pair_mine = lax.dynamic_index_in_dim(pair, chip, 0, keepdims=False)
    pair_other = lax.dynamic_index_in_dim(pair, 1 - chip, 0, keepdims=False)
    total = pair_mine + swap(pair_other.astype(BF16), 2).astype(F32)

    sent = total.astype(BF16).reshape(blocks, group, columns)
    sent, total = lax.optimization_barrier((sent, total))
    inner_total = exchange(sent)

    copy = (state_rows.astype(F32) + 0.3325 * total).astype(BF16)
    beside = swap(copy, 1)
    across = swap(copy, 2)
    diagonal = swap(across, 1)
    pseudo_grad = outer_here - inner_total.astype(F32) / replicas
    new_momentum = 0.9 * momentum_here + pseudo_grad
    new_outer = outer_here - 0.7 * (pseudo_grad + 0.9 * new_momentum)
    mixed = mix(rep, shard, [copy, beside, across, diagonal])
    return (mixed[None], new_outer[:, None], new_momentum[:, None])


def solution(mesh):
    in_specs = (
        P("rep", "fsdp", "tp"),
        P(None, ("rep", "fsdp"), None, "tp"),
        P(None, ("rep", "fsdp"), None, "tp"),
    )
    out_specs = (
        P("rep", "fsdp", "tp"),
        P(None, ("rep", "fsdp"), None, "tp"),
        P(None, ("rep", "fsdp"), None, "tp"),
    )
    return jax.shard_map(
        on_device, mesh=mesh, in_specs=in_specs, out_specs=out_specs, check_vma=False
    )
```

time: 91.1 us -> 76.6 us (0.84)
  the two profiles are of different devices: /device:TPU:1 before, /device:TPU:24 now
where the time goes in v3:
time: 76.6 us; the launch traced here: 76.2 us
  waiting for transfers between devices  35.9 us (47%)
  starting transfers between devices  32.6 us (43%)
  other arithmetic  4.52 us (6%)
  Pallas kernels  1.35 us (2%)
  local copies, waits for them, and re-layouts  1.06 us (1%)
  between operations  0.81 us (1%)
    all_to_all x2, starting transfers between devices, exchange(): lax.all_to_all(value, 'fsdp', split_axis=0, concat_axis=0, tiled=True)  21.8 us
    all_to_all x2, waiting for transfers between devices, exchange(): lax.all_to_all(value, 'fsdp', split_axis=0, concat_axis=0, tiled=True)  19.3 us
    ppermute x5, waiting for transfers between devices, swap(): return lax.ppermute(value, 'rep', [(r, r ^ i) for r in range(replicas)])  16.6 us
    ppermute x5, starting transfers between devices, swap(): return lax.ppermute(value, 'rep', [(r, r ^ i) for r in range(replicas)])  10.8 us
    convert_element_type x1, other arithmetic, on_device(): state_part = (-0.33 * outer_here - 0.567 * momentum_here).astype(BF16)  2.49 us
    broadcast_in_dim x1, other arithmetic, on_device(): return (mixed[None], new_outer[:, None], new_momentum[:, None])  1.78 us
  transfers between devices with their start and end apart: 7, of which 5 were waited for; matrix products, arithmetic and copies ran while one was open for 2% of the time, Pallas kernels for 2%

profile of v3, /device:TPU:24, one launch (start us, length us, event | category | flops | bytes accessed | tf_op | source)
XLA Modules:
  0.0 76.2 jit_solution(5561856943201921663)
XLA Ops:
  0.6 0.0 copy-start
  0.7 2.5 %fusion = bf16[32,2,2048]{2,1,0:T(2,128)(2,1)} fusion(f32[32,1,2,2048]{3,2,1,0:T(2,128)} %param.5, f32[32,1,2,2048]{3,2,1,0:T(2,128)} %param.4), kind=kLoop, calls=%fused_computation.4 | loop fusion | flops 524288 | bytes 1310720 | tf_op jit(solution)/shard_map/convert_element_type | solution.py:57
  3.1 0.0 copy-done
  3.2 1.9 %collective-permute-start = (bf16[2,64,2048]{2,1,0:T(8,128)(2,1)S(1)}, bf16[2,64,2048]{2,1,0:T(8,128)(2,1)S(1)}, u32[]{:S(2)}, u32[]{:S(2)}) collective-permute-start(bf16[2,64,2048]{2,1,0:T(8,128)(2,1)S(1)} %dynamic-slice_bitcast_fusion), channel_id=1, source_target_pairs={{0,128},{128,0},{256,384},{384,256},{1,129},{129,1},{257,385},{385... | collective-permute-start | bytes 1572872 | tf_op jit(solution)/shard_map/ppermute | solution.py:55
  5.1 18.0 %all-to-all-start = ((bf16[32,2,2048]{2,1,0:T(2,128)(2,1)}), bf16[32,2,2048]{2,1,0:T(2,128)(2,1)S(1)}, u32[]{:S(2)}, u32[]{:S(2)}) async-start(bf16[32,2,2048]{2,1,0:T(2,128)(2,1)} %fusion), calls=%async_computation | async-start | bytes 524288 | tf_op jit(solution)/shard_map/all_to_all | solution.py:52
  23.1 0.0 collective-permute-done
  23.1 0.1 convert_add_fusion
  23.3 2.5 %collective-permute-start.1 = (bf16[64,2048]{1,0:T(8,128)(2,1)S(1)}, bf16[64,2048]{1,0:T(8,128)(2,1)S(1)}, u32[]{:S(2)}, u32[]{:S(2)}) collective-permute-start(bf16[64,2048]{1,0:T(8,128)(2,1)S(1)} %fusion.2), channel_id=1, source_target_pairs={{0,256},{128,384},{256,0},{384,128},{1,257},{129,385},{257,1},{385... | collective-permute-start | bytes 786440 | tf_op jit(solution)/shard_map/ppermute | solution.py:55
  25.8 9.5 %collective-permute-done.1 = bf16[64,2048]{1,0:T(8,128)(2,1)S(1)} collective-permute-done((bf16[64,2048]{1,0:T(8,128)(2,1)S(1)}, bf16[64,2048]{1,0:T(8,128)(2,1)S(1)}, u32[]{:S(2)}, u32[]{:S(2)}) %collective-permute-start.1) | collective-permute-done | bytes 262176 | tf_op jit(solution)/shard_map/ppermute | solution.py:55
  35.3 0.1 fusion.4
  35.4 0.9 %reshape.23 = bf16[32,2,2048]{2,1,0:T(2,128)(2,1)} reshape(bf16[64,2048]{1,0:T(8,128)(2,1)S(1)} %get-tuple-element.11) | data formatting | bytes 524288 | tf_op jit(solution)/shard_map/reshape | solution.py:69
  36.3 11.2 %all-to-all-done = bf16[32,2,2048]{2,1,0:T(2,128)(2,1)S(1)} async-done(((bf16[32,2,2048]{2,1,0:T(2,128)(2,1)}), bf16[32,2,2048]{2,1,0:T(2,128)(2,1)S(1)}, u32[]{:S(2)}, u32[]{:S(2)}) %all-to-all-start) | async-done | bytes 262176 | tf_op jit(solution)/shard_map/all_to_all | solution.py:52
  47.5 3.9 %all-to-all-start.1 = ((bf16[32,2,2048]{2,1,0:T(2,128)(2,1)}), bf16[32,2,2048]{2,1,0:T(2,128)(2,1)S(1)}, u32[]{:S(2)}, u32[]{:S(2)}) async-start(bf16[32,2,2048]{2,1,0:T(2,128)(2,1)} %reshape.23), calls=%async_computation.1 | async-start | bytes 524288 | tf_op jit(solution)/shard_map/all_to_all | solution.py:52
  51.4 0.1 reshape.24
  51.4 0.1 add_convert_fusion.refs_0_
  51.5 2.5 %collective-permute-start.3 = (bf16[64,2048]{1,0:T(8,128)(2,1)S(1)}, bf16[64,2048]{1,0:T(8,128)(2,1)S(1)}, u32[]{:S(2)}, u32[]{:S(2)}) collective-permute-start(bf16[64,2048]{1,0:T(8,128)(2,1)S(1)} %add_convert_fusion.refs_0_), channel_id=1, source_target_pairs={{0,256},{128,384},{256,0},{384,128},{1,257},{129,385},{257,1},{385... | collective-permute-start | bytes 786440 | tf_op jit(solution)/shard_map/ppermute | solution.py:55
  54.0 1.9 %collective-permute-start.2 = (bf16[64,2048]{1,0:T(8,128)(2,1)S(1)}, bf16[64,2048]{1,0:T(8,128)(2,1)S(1)}, u32[]{:S(2)}, u32[]{:S(2)}) collective-permute-start(bf16[64,2048]{1,0:T(8,128)(2,1)S(1)} %add_convert_fusion.refs_0_), channel_id=1, source_target_pairs={{0,128},{128,0},{256,384},{384,256},{1,129},{129,1},{257,385},{385... | collective-permute-start | bytes 786440 | tf_op jit(solution)/shard_map/ppermute | solution.py:55
  55.9 5.6 %collective-permute-done.3.refs_2_ = bf16[64,2048]{1,0:T(8,128)(2,1)S(1)} collective-permute-done((bf16[64,2048]{1,0:T(8,128)(2,1)S(1)}, bf16[64,2048]{1,0:T(8,128)(2,1)S(1)}, u32[]{:S(2)}, u32[]{:S(2)}) %collective-permute-start.3) | collective-permute-done | bytes 262176 | tf_op jit(solution)/shard_map/ppermute | solution.py:55
  61.5 1.9 %collective-permute-start.4 = (bf16[64,2048]{1,0:T(8,128)(2,1)S(1)}, bf16[64,2048]{1,0:T(8,128)(2,1)S(1)}, u32[]{:S(2)}, u32[]{:S(2)}) collective-permute-start(bf16[64,2048]{1,0:T(8,128)(2,1)S(1)} %collective-permute-done.3.refs_2_), channel_id=1, source_target_pairs={{0,128},{128,0},{256,384},{384,256},{1,129},{129,1},{257,385},{385... | collective-permute-start | bytes 786440 | tf_op jit(solution)/shard_map/ppermute | solution.py:55
  63.5 0.0 collective-permute-done.2.refs_1_
  63.5 1.5 %collective-permute-done.4.refs_3_ = bf16[64,2048]{1,0:T(8,128)(2,1)S(1)} collective-permute-done((bf16[64,2048]{1,0:T(8,128)(2,1)S(1)}, bf16[64,2048]{1,0:T(8,128)(2,1)S(1)}, u32[]{:S(2)}, u32[]{:S(2)}) %collective-permute-start.4) | collective-permute-done | bytes 262176 | tf_op jit(solution)/shard_map/ppermute | solution.py:55
  65.0 0.0 copy-start.1
  65.0 0.0 copy-start.2
  65.0 1.3 %shard_map.58 = bf16[256,2048]{1,0:T(8,128)(2,1)} custom-call(s32[1]{0:T(128)} %bitcast.rep_ref, bf16[256,2048]{1,0:T(8,128)(2,1)S(1)} %bitcast.57, bf16[64,2048]{1,0:T(8,128)(2,1)S(1)} %add_convert_fusion.refs_0_, bf16[64,2048]{1,0:T(8,128)(2,1)S(1)} %collective-permute-done.2.refs_1_, bf16[64,2048]{1,0:T(8,128)(2,1)S(1)} %collective-permute-done.3.refs_2_, ...), custom_call_target="tpu_custom_call" | custom-call | bytes 3145728 | tf_op jit(solution)/shard_map/pallas_call | solution.py:29
  66.3 8.1 %all-to-all-done.1 = bf16[32,2,2048]{2,1,0:T(2,128)(2,1)S(1)} async-done(((bf16[32,2,2048]{2,1,0:T(2,128)(2,1)}), bf16[32,2,2048]{2,1,0:T(2,128)(2,1)S(1)}, u32[]{:S(2)}, u32[]{:S(2)}) %all-to-all-start.1) | async-done | bytes 262176 | tf_op jit(solution)/shard_map/all_to_all | solution.py:52
  74.4 0.0 copy-done.1
  74.4 0.0 copy-done.2
  74.4 1.8 %fusion.3 = (f32[32,1,2,2048]{3,2,1,0:T(2,128)}, f32[32,1,2,2048]{3,2,1,0:T(2,128)}) fusion(bf16[32,2,2048]{2,1,0:T(2,128)(2,1)S(1)} %all-to-all-done.1, f32[32,1,2,2048]{3,2,1,0:T(2,128)S(1)} %copy-done.2, f32[32,1,2,2048]{3,2,1,0:T(2,128)S(1)} %copy-done.1), kind=kLoop, calls=%fused_computation.15 | loop fusion | flops 1179648 | bytes 2359296 | tf_op jit(solution)/shard_map/broadcast_in_dim | solution.py:81
  (2 shorter events, 0.1 us)
Async XLA Ops:
  0.6 2.5 %copy-start = (bf16[1,256,2048]{2,1,0:T(8,128)(2,1)S(1)}, bf16[1,256,2048]{2,1,0:T(8,128)(2,1)}, u32[]{:S(2)}) copy-start(bf16[1,256,2048]{2,1,0:T(8,128)(2,1)} %param.3) | copy-start | bytes 3145732
  3.2 19.9 %collective-permute-start = (bf16[2,64,2048]{2,1,0:T(8,128)(2,1)S(1)}, bf16[2,64,2048]{2,1,0:T(8,128)(2,1)S(1)}, u32[]{:S(2)}, u32[]{:S(2)}) collective-permute-start(bf16[2,64,2048]{2,1,0:T(8,128)(2,1)S(1)} %dynamic-slice_bitcast_fusion), channel_id=1, source_target_pairs={{0,128},{128,0},{256,384},{384,256},{1,129},{129,1},{257,385},{385... | collective-permute-start | bytes 1572872 | tf_op jit(solution)/shard_map/ppermute | solution.py:55
  5.1 42.3 %all-to-all-start = ((bf16[32,2,2048]{2,1,0:T(2,128)(2,1)}), bf16[32,2,2048]{2,1,0:T(2,128)(2,1)S(1)}, u32[]{:S(2)}, u32[]{:S(2)}) async-start(bf16[32,2,2048]{2,1,0:T(2,128)(2,1)} %fusion), calls=%async_computation | async-start | bytes 524288 | tf_op jit(solution)/shard_map/all_to_all | solution.py:52
  23.3 12.0 %collective-permute-start.1 = (bf16[64,2048]{1,0:T(8,128)(2,1)S(1)}, bf16[64,2048]{1,0:T(8,128)(2,1)S(1)}, u32[]{:S(2)}, u32[]{:S(2)}) collective-permute-start(bf16[64,2048]{1,0:T(8,128)(2,1)S(1)} %fusion.2), channel_id=1, source_target_pairs={{0,256},{128,384},{256,0},{384,128},{1,257},{129,385},{257,1},{385... | collective-permute-start | bytes 786440 | tf_op jit(solution)/shard_map/ppermute | solution.py:55
  47.5 26.9 %all-to-all-start.1 = ((bf16[32,2,2048]{2,1,0:T(2,128)(2,1)}), bf16[32,2,2048]{2,1,0:T(2,128)(2,1)S(1)}, u32[]{:S(2)}, u32[]{:S(2)}) async-start(bf16[32,2,2048]{2,1,0:T(2,128)(2,1)} %reshape.23), calls=%async_computation.1 | async-start | bytes 524288 | tf_op jit(solution)/shard_map/all_to_all | solution.py:52
  51.5 10.0 %collective-permute-start.3 = (bf16[64,2048]{1,0:T(8,128)(2,1)S(1)}, bf16[64,2048]{1,0:T(8,128)(2,1)S(1)}, u32[]{:S(2)}, u32[]{:S(2)}) collective-permute-start(bf16[64,2048]{1,0:T(8,128)(2,1)S(1)} %add_convert_fusion.refs_0_), channel_id=1, source_target_pairs={{0,256},{128,384},{256,0},{384,128},{1,257},{129,385},{257,1},{385... | collective-permute-start | bytes 786440 | tf_op jit(solution)/shard_map/ppermute | solution.py:55
  54.0 9.4 %collective-permute-start.2 = (bf16[64,2048]{1,0:T(8,128)(2,1)S(1)}, bf16[64,2048]{1,0:T(8,128)(2,1)S(1)}, u32[]{:S(2)}, u32[]{:S(2)}) collective-permute-start(bf16[64,2048]{1,0:T(8,128)(2,1)S(1)} %add_convert_fusion.refs_0_), channel_id=1, source_target_pairs={{0,128},{128,0},{256,384},{384,256},{1,129},{129,1},{257,385},{385... | collective-permute-start | bytes 786440 | tf_op jit(solution)/shard_map/ppermute | solution.py:55
  61.5 3.4 %collective-permute-start.4 = (bf16[64,2048]{1,0:T(8,128)(2,1)S(1)}, bf16[64,2048]{1,0:T(8,128)(2,1)S(1)}, u32[]{:S(2)}, u32[]{:S(2)}) collective-permute-start(bf16[64,2048]{1,0:T(8,128)(2,1)S(1)} %collective-permute-done.3.refs_2_), channel_id=1, source_target_pairs={{0,128},{128,0},{256,384},{384,256},{1,129},{129,1},{257,385},{385... | collective-permute-start | bytes 786440 | tf_op jit(solution)/shard_map/ppermute | solution.py:55
  65.0 9.4 %copy-start.1 = (f32[32,1,2,2048]{3,2,1,0:T(2,128)S(1)}, f32[32,1,2,2048]{3,2,1,0:T(2,128)}, u32[]{:S(2)}) copy-start(f32[32,1,2,2048]{3,2,1,0:T(2,128)} %param.5) | copy-start | bytes 1572868
  65.0 9.4 %copy-start.2 = (f32[32,1,2,2048]{3,2,1,0:T(2,128)S(1)}, f32[32,1,2,2048]{3,2,1,0:T(2,128)}, u32[]{:S(2)}) copy-start(f32[32,1,2,2048]{3,2,1,0:T(2,128)} %param.4) | copy-start | bytes 1572868

commit v4 on v3

--- a/solution.py
+++ b/solution.py
@@ -8,11 +8,89 @@
 F32 = jnp.float32
 BF16 = jnp.bfloat16
 VMEM = pl.BlockSpec(memory_space=pltpu.VMEM)
+SMEM = pl.BlockSpec(memory_space=pltpu.SMEM)
+ANY = pl.BlockSpec(memory_space=pl.ANY)
 PARAMS = pltpu.CompilerParams(vmem_limit_bytes=32 * 1024 * 1024)
+FIRST = 11
 
 
 def cost(nbytes):
     return pl.CostEstimate(flops=0, bytes_accessed=nbytes, transcendentals=0)
+
+
+def segments(blocks):
+    ring = blocks // 2
+    late = ring - FIRST
+    for half in (0, ring):
+        yield half, half + FIRST, late
+        yield half + late, half, FIRST
+
+
+def first_kernel(chip_ref, weights_ref, momentum_ref, parts_ref, state_ref, other_ref, *scratch):
+    weights, momentum, state, sems = scratch
+    other = pltpu.make_async_copy(parts_ref.at[1 - chip_ref[0]], other_ref, sems.at[3, 0])
+    runs = list(segments(weights.shape[0]))
+    loads, stores = [], []
+    for n, (place, index, length) in enumerate(runs):
+        rows = pl.ds(index, length)
+        for m, (source, target) in enumerate(((weights_ref, weights), (momentum_ref, momentum))):
+            copy = pltpu.make_async_copy(source.at[rows], target.at[rows], sems.at[m, n])
+            copy.start()
+            loads.append(copy)
+        if n == 0:
+            other.start()
+    for n, (place, index, length) in enumerate(runs):
+        loads[2 * n].wait()
+        loads[2 * n + 1].wait()
+        rows, places = pl.ds(index, length), pl.ds(place, length)
+        state[places] = (-0.33 * weights[rows] - 0.567 * momentum[rows]).astype(BF16)
+        copy = pltpu.make_async_copy(state.at[places], state_ref.at[places], sems.at[2, n])
+        copy.start()
+        stores.append(copy)
+    other.wait()
+    for copy in stores:
+        copy.wait()
+
+
+def state_and_other(chip, weights, momentum, parts):
+    shape = weights.shape
+    return pl.pallas_call(
+        first_kernel,
+        in_specs=[SMEM, ANY, ANY, ANY],
+        out_specs=[ANY, VMEM],
+        out_shape=[
+            jax.ShapeDtypeStruct(shape, BF16),
+            jax.ShapeDtypeStruct(parts.shape[1:], BF16),
+        ],
+        scratch_shapes=[
+            pltpu.VMEM(shape, F32),
+            pltpu.VMEM(shape, F32),
+            pltpu.VMEM(shape, BF16),
+            pltpu.SemaphoreType.DMA((4, 4)),
+        ],
+        cost_estimate=cost(3 << 20),
+    )(chip.reshape(1), weights, momentum, parts)
+
+
+def update_kernel(total_ref, weights_ref, momentum_ref, outer_ref, out_momentum_ref):
+    for place, index, length in segments(weights_ref.shape[0]):
+        rows = pl.ds(index, length)
+        weights = weights_ref[rows]
+        pseudo_grad = weights - 0.25 * total_ref[pl.ds(place, length)].astype(F32)
+        momentum = 0.9 * momentum_ref[rows] + pseudo_grad
+        out_momentum_ref[rows] = momentum
+        outer_ref[rows] = weights - 0.7 * (pseudo_grad + 0.9 * momentum)
+
+
+def update(total, weights, momentum):
+    return pl.pallas_call(
+        update_kernel,
+        in_specs=[VMEM] * 3,
+        out_specs=[VMEM] * 2,
+        out_shape=[jax.ShapeDtypeStruct(weights.shape, F32)] * 2,
+        cost_estimate=cost(3 << 20),
+        compiler_params=PARAMS,
+    )(total, weights, momentum)
 
 
 def mix_kernel(rep_ref, shard_ref, *refs):
@@ -28,7 +106,7 @@
 def mix(rep, shard, copies):
     return pl.pallas_call(
         mix_kernel,
-        in_specs=[pl.BlockSpec(memory_space=pltpu.SMEM)] + [VMEM] * (1 + len(copies)),
+        in_specs=[SMEM] + [VMEM] * (1 + len(copies)),
         out_specs=VMEM,
         out_shape=jax.ShapeDtypeStruct(shard.shape, BF16),
         cost_estimate=cost(3 << 20),
@@ -47,26 +125,33 @@
     chip, core = rep // 2, rep % 2
     outer_here = outer_weights[:, 0]
     momentum_here = outer_momentum[:, 0]
+    ring = blocks // 2
+    order = [half + (FIRST + z) % ring for half in (0, ring) for z in range(ring)]
 
     def exchange(value):
-        return lax.all_to_all(value, "fsdp", split_axis=0, concat_axis=0, tiled=True)
+        return lax.all_to_all(
+            value, "fsdp", split_axis=0, concat_axis=0, axis_index_groups=[order], tiled=True
+        )
+
+    def turn(value, by):
+        halves = value.reshape(2, ring, *value.shape[1:])
+        halves = jnp.concatenate([halves[:, by:], halves[:, :by]], axis=1)
+        return halves.reshape(value.shape)
 
     def swap(value, i):
         return lax.ppermute(value, "rep", [(r, r ^ i) for r in range(replicas)])
 
-    state_part = (-0.33 * outer_here - 0.567 * momentum_here).astype(BF16)
-    parts = shard.reshape(2, 2, quarter, columns)
-    parts, state_part = lax.optimization_barrier((parts, state_part))
-    state_rows = exchange(state_part).reshape(quarter, columns)
+    parts = shard.reshape(2, 2 * quarter, columns)
+    state_part, other = state_and_other(chip, outer_here, momentum_here, parts)
+    state_rows = turn(exchange(state_part), ring - FIRST).reshape(quarter, columns)
 
-    other = lax.dynamic_index_in_dim(parts, 1 - core, 1, keepdims=False)
-    mine = lax.dynamic_index_in_dim(parts, core, 1, keepdims=False)
-    pair = mine.astype(F32) + swap(other, 1).astype(F32)
-    pair_mine = lax.dynamic_index_in_dim(pair, chip, 0, keepdims=False)
-    pair_other = lax.dynamic_index_in_dim(pair, 1 - chip, 0, keepdims=False)
-    total = pair_mine + swap(pair_other.astype(BF16), 2).astype(F32)
+    mine = lax.dynamic_index_in_dim(parts, chip, 0, keepdims=False)
+    pair = (mine.astype(F32) + swap(other, 2).astype(F32)).reshape(2, quarter, columns)
+    pair_mine = lax.dynamic_index_in_dim(pair, core, 0, keepdims=False)
+    pair_other = lax.dynamic_index_in_dim(pair, 1 - core, 0, keepdims=False)
+    total = pair_mine + swap(pair_other.astype(BF16), 1).astype(F32)
 
-    sent = total.astype(BF16).reshape(blocks, group, columns)
+    sent = turn(total.astype(BF16).reshape(blocks, group, columns), FIRST)
     sent, total = lax.optimization_barrier((sent, total))
     inner_total = exchange(sent)
 
@@ -74,10 +159,9 @@
     beside = swap(copy, 1)
     across = swap(copy, 2)
     diagonal = swap(across, 1)
-    pseudo_grad = outer_here - inner_total.astype(F32) / replicas
-    new_momentum = 0.9 * momentum_here + pseudo_grad
-    new_outer = outer_here - 0.7 * (pseudo_grad + 0.9 * new_momentum)
     mixed = mix(rep, shard, [copy, beside, across, diagonal])
+
+    new_outer, new_momentum = update(inner_total, outer_here, momentum_here)
     return (mixed[None], new_outer[:, None], new_momentum[:, None])
 
 

time: 76.6 us -> 70.6 us (0.922)
  the two profiles are of different devices: /device:TPU:24 before, /device:TPU:1 now
where the time goes in v4:
time: 70.6 us; the launch traced here: 70.2 us
  starting transfers between devices  49.2 us (70%)
  waiting for transfers between devices  12 us (17%)
  Pallas kernels  5.59 us (8%)
  other arithmetic  1.58 us (2%)
  local copies, waits for them, and re-layouts  0.97 us (1%)
  between operations  0.86 us (1%)
    all_to_all x2, starting transfers between devices, exchange(): lax.all_to_all(value, 'fsdp', split_axis=0, concat_axis=0, axis_index_gro...  29.7 us
    ppermute x5, starting transfers between devices, swap(): return lax.ppermute(value, 'rep', [(r, r ^ i) for r in range(replicas)])  19.5 us
    all_to_all x2, waiting for transfers between devices, exchange(): lax.all_to_all(value, 'fsdp', split_axis=0, concat_axis=0, axis_index_gro...  7.77 us
    ppermute x5, waiting for transfers between devices, swap(): return lax.ppermute(value, 'rep', [(r, r ^ i) for r in range(replicas)])  4.22 us
    pallas_call x1, Pallas kernels, state_and_other(): pl.pallas_call(first_kernel, in_specs=[SMEM, ANY, ANY, ANY], out_specs=[A...  3.12 us
  transfers between devices with their start and end apart: 7, of which 4 were waited for; matrix products, arithmetic and copies ran while one was open for 4% of the time, Pallas kernels for 2%

profile of v4, /device:TPU:1, one launch (start us, length us, event | category | flops | bytes accessed | tf_op | source)
XLA Modules:
  0.0 70.2 jit_solution(7724922512758674136)
XLA Ops:
  0.6 0.0 copy-start
  0.7 3.1 %shard_map.58 = (bf16[32,2,2048]{2,1,0:T(2,128)(2,1)}, bf16[128,2048]{1,0:T(8,128)(2,1)}) custom-call(s32[1]{0:T(128)} %bitcast.2.chip_ref, f32[32,2,2048]{2,1,0:T(2,128)} %bitcast.27, f32[32,2,2048]{2,1,0:T(2,128)} %bitcast.29, bf16[2,128,2048]{2,1,0:T(8,128)(2,1)} %bitcast.24), custom_call_target="tpu_custom_call" | custom-call | bytes 3145728 | tf_op jit(solution)/shard_map/pallas_call | solution.py:57
  3.8 3.9 %collective-permute-start = (bf16[128,2048]{1,0:T(8,128)(2,1)}, bf16[128,2048]{1,0:T(8,128)(2,1)S(1)}, u32[]{:S(2)}, u32[]{:S(2)}) collective-permute-start(bf16[128,2048]{1,0:T(8,128)(2,1)} %get-tuple-element.10), channel_id=1, source_target_pairs={{0,256},{128,384},{256,0},{384,128},{1,257},{129,385},{257,1},{385... | collective-permute-start | bytes 1572872 | tf_op jit(solution)/shard_map/ppermute | solution.py:142
  7.7 17.9 %all-to-all-start = ((bf16[32,2,2048]{2,1,0:T(2,128)(2,1)}), bf16[32,2,2048]{2,1,0:T(2,128)(2,1)S(1)}, u32[]{:S(2)}, u32[]{:S(2)}) async-start(bf16[32,2,2048]{2,1,0:T(2,128)(2,1)} %get-tuple-element.9), calls=%async_computation | async-start | bytes 524288 | tf_op jit(solution)/shard_map/all_to_all | solution.py:132
  25.7 0.0 collective-permute-done
  25.7 0.0 copy-done
  25.7 0.1 convert_add_fusion
  25.9 3.4 %collective-permute-start.1 = (bf16[64,2048]{1,0:T(8,128)(2,1)S(1)}, bf16[64,2048]{1,0:T(8,128)(2,1)S(1)}, u32[]{:S(2)}, u32[]{:S(2)}) collective-permute-start(bf16[64,2048]{1,0:T(8,128)(2,1)S(1)} %fusion), channel_id=1, source_target_pairs={{0,128},{128,0},{256,384},{384,256},{1,129},{129,1},{257,385},{385... | collective-permute-start | bytes 786440 | tf_op jit(solution)/shard_map/ppermute | solution.py:142
  29.3 1.1 %collective-permute-done.1 = bf16[64,2048]{1,0:T(8,128)(2,1)S(1)} collective-permute-done((bf16[64,2048]{1,0:T(8,128)(2,1)S(1)}, bf16[64,2048]{1,0:T(8,128)(2,1)S(1)}, u32[]{:S(2)}, u32[]{:S(2)}) %collective-permute-start.1) | collective-permute-done | bytes 262176 | tf_op jit(solution)/shard_map/ppermute | solution.py:142
  30.5 0.1 fusion.1
  30.5 0.2 reshape_reshape.4
  30.7 0.1 slice.19
  30.9 0.1 slice.18
  30.9 1.0 %pad_maximum_fusion = bf16[2,16,2,2048]{3,2,1,0:T(2,128)(2,1)} fusion(bf16[2,11,2,2048]{3,2,1,0:T(2,128)(2,1)S(1)} %slice.19, bf16[2,5,2,2048]{3,2,1,0:T(2,128)(2,1)S(1)} %slice.18), kind=kLoop, calls=%fused_computation.6 | loop fusion | flops 131072 | bytes 524288 | tf_op jit(solution)/shard_map/concatenate | solution.py:138
  32.0 7.8 %all-to-all-done = bf16[32,2,2048]{2,1,0:T(2,128)(2,1)S(1)} async-done(((bf16[32,2,2048]{2,1,0:T(2,128)(2,1)}), bf16[32,2,2048]{2,1,0:T(2,128)(2,1)S(1)}, u32[]{:S(2)}, u32[]{:S(2)}) %all-to-all-start) | async-done | bytes 262176 | tf_op jit(solution)/shard_map/all_to_all | solution.py:132
  39.7 11.8 %all-to-all-start.1 = ((bf16[32,2,2048]{2,1,0:T(2,128)(2,1)}), bf16[32,2,2048]{2,1,0:T(2,128)(2,1)S(1)}, u32[]{:S(2)}, u32[]{:S(2)}) async-start(bf16[32,2,2048]{2,1,0:T(2,128)(2,1)} %bitcast.11), calls=%async_computation.1 | async-start | bytes 524288 | tf_op jit(solution)/shard_map/all_to_all | solution.py:132
  51.5 0.1 slice.16
  51.7 0.1 slice.17
  51.7 0.3 maximum_convert_fusion
  52.0 0.4 reshape.31
  52.4 0.1 add_convert_fusion.refs_0_
  52.5 1.9 %collective-permute-start.3 = (bf16[64,2048]{1,0:T(8,128)(2,1)S(1)}, bf16[64,2048]{1,0:T(8,128)(2,1)S(1)}, u32[]{:S(2)}, u32[]{:S(2)}) collective-permute-start(bf16[64,2048]{1,0:T(8,128)(2,1)S(1)} %add_convert_fusion.refs_0_), channel_id=1, source_target_pairs={{0,256},{128,384},{256,0},{384,128},{1,257},{129,385},{257,1},{385... | collective-permute-start | bytes 786440 | tf_op jit(solution)/shard_map/ppermute | solution.py:142
  54.4 5.0 %collective-permute-start.2 = (bf16[64,2048]{1,0:T(8,128)(2,1)S(1)}, bf16[64,2048]{1,0:T(8,128)(2,1)S(1)}, u32[]{:S(2)}, u32[]{:S(2)}) collective-permute-start(bf16[64,2048]{1,0:T(8,128)(2,1)S(1)} %add_convert_fusion.refs_0_), channel_id=1, source_target_pairs={{0,128},{128,0},{256,384},{384,256},{1,129},{129,1},{257,385},{385... | collective-permute-start | bytes 786440 | tf_op jit(solution)/shard_map/ppermute | solution.py:142
  59.4 2.0 %collective-permute-done.3.refs_2_ = bf16[64,2048]{1,0:T(8,128)(2,1)S(1)} collective-permute-done((bf16[64,2048]{1,0:T(8,128)(2,1)S(1)}, bf16[64,2048]{1,0:T(8,128)(2,1)S(1)}, u32[]{:S(2)}, u32[]{:S(2)}) %collective-permute-start.3) | collective-permute-done | bytes 262176 | tf_op jit(solution)/shard_map/ppermute | solution.py:142
  61.4 5.2 %collective-permute-start.4 = (bf16[64,2048]{1,0:T(8,128)(2,1)S(1)}, bf16[64,2048]{1,0:T(8,128)(2,1)S(1)}, u32[]{:S(2)}, u32[]{:S(2)}) collective-permute-start(bf16[64,2048]{1,0:T(8,128)(2,1)S(1)} %collective-permute-done.3.refs_2_), channel_id=1, source_target_pairs={{0,128},{128,0},{256,384},{384,256},{1,129},{129,1},{257,385},{385... | collective-permute-start | bytes 786440 | tf_op jit(solution)/shard_map/ppermute | solution.py:142
  66.6 0.0 collective-permute-done.2.refs_1_
  66.6 1.1 %collective-permute-done.4.refs_3_ = bf16[64,2048]{1,0:T(8,128)(2,1)S(1)} collective-permute-done((bf16[64,2048]{1,0:T(8,128)(2,1)S(1)}, bf16[64,2048]{1,0:T(8,128)(2,1)S(1)}, u32[]{:S(2)}, u32[]{:S(2)}) %collective-permute-start.4) | collective-permute-done | bytes 262176 | tf_op jit(solution)/shard_map/ppermute | solution.py:142
  67.7 0.0 copy-start.1
  67.7 0.0 copy-start.2
  67.7 1.3 %shard_map.59 = bf16[256,2048]{1,0:T(8,128)(2,1)} custom-call(s32[1]{0:T(128)} %bitcast.rep_ref, bf16[256,2048]{1,0:T(8,128)(2,1)S(1)} %bitcast.26, bf16[64,2048]{1,0:T(8,128)(2,1)S(1)} %add_convert_fusion.refs_0_, bf16[64,2048]{1,0:T(8,128)(2,1)S(1)} %collective-permute-done.2.refs_1_, bf16[64,2048]{1,0:T(8,128)(2,1)S(1)} %collective-permute-done.3.refs_2_, ...), custom_call_target="tpu_custom_call" | custom-call | bytes 3145728 | tf_op jit(solution)/shard_map/pallas_call | solution.py:107
  69.1 0.0 all-to-all-done.1.total_ref
  69.1 0.0 copy-done.1
  69.1 0.0 copy-done.2
  69.1 1.1 %shard_map.60 = (f32[32,2,2048]{2,1,0:T(2,128)}, f32[32,2,2048]{2,1,0:T(2,128)}) custom-call(bf16[32,2,2048]{2,1,0:T(2,128)(2,1)S(1)} %all-to-all-done.1.total_ref, f32[32,2,2048]{2,1,0:T(2,128)S(1)} %bitcast.28, f32[32,2,2048]{2,1,0:T(2,128)S(1)} %bitcast.30), custom_call_target="tpu_custom_call" | custom-call | bytes 3145728 | tf_op jit(solution)/shard_map/pallas_call | solution.py:86
  (1 shorter events, 0.0 us)
Async XLA Ops:
  0.6 25.1 %copy-start = (bf16[1,256,2048]{2,1,0:T(8,128)(2,1)S(1)}, bf16[1,256,2048]{2,1,0:T(8,128)(2,1)}, u32[]{:S(2)}) copy-start(bf16[1,256,2048]{2,1,0:T(8,128)(2,1)} %param.3) | copy-start | bytes 3145732
  3.8 21.9 %collective-permute-start = (bf16[128,2048]{1,0:T(8,128)(2,1)}, bf16[128,2048]{1,0:T(8,128)(2,1)S(1)}, u32[]{:S(2)}, u32[]{:S(2)}) collective-permute-start(bf16[128,2048]{1,0:T(8,128)(2,1)} %get-tuple-element.10), channel_id=1, source_target_pairs={{0,256},{128,384},{256,0},{384,128},{1,257},{129,385},{257,1},{385... | collective-permute-start | bytes 1572872 | tf_op jit(solution)/shard_map/ppermute | solution.py:142
  7.7 32.0 %all-to-all-start = ((bf16[32,2,2048]{2,1,0:T(2,128)(2,1)}), bf16[32,2,2048]{2,1,0:T(2,128)(2,1)S(1)}, u32[]{:S(2)}, u32[]{:S(2)}) async-start(bf16[32,2,2048]{2,1,0:T(2,128)(2,1)} %get-tuple-element.9), calls=%async_computation | async-start | bytes 524288 | tf_op jit(solution)/shard_map/all_to_all | solution.py:132
  25.9 4.6 %collective-permute-start.1 = (bf16[64,2048]{1,0:T(8,128)(2,1)S(1)}, bf16[64,2048]{1,0:T(8,128)(2,1)S(1)}, u32[]{:S(2)}, u32[]{:S(2)}) collective-permute-start(bf16[64,2048]{1,0:T(8,128)(2,1)S(1)} %fusion), channel_id=1, source_target_pairs={{0,128},{128,0},{256,384},{384,256},{1,129},{129,1},{257,385},{385... | collective-permute-start | bytes 786440 | tf_op jit(solution)/shard_map/ppermute | solution.py:142
  39.7 29.4 %all-to-all-start.1 = ((bf16[32,2,2048]{2,1,0:T(2,128)(2,1)}), bf16[32,2,2048]{2,1,0:T(2,128)(2,1)S(1)}, u32[]{:S(2)}, u32[]{:S(2)}) async-start(bf16[32,2,2048]{2,1,0:T(2,128)(2,1)} %bitcast.11), calls=%async_computation.1 | async-start | bytes 524288 | tf_op jit(solution)/shard_map/all_to_all | solution.py:132
  52.5 8.9 %collective-permute-start.3 = (bf16[64,2048]{1,0:T(8,128)(2,1)S(1)}, bf16[64,2048]{1,0:T(8,128)(2,1)S(1)}, u32[]{:S(2)}, u32[]{:S(2)}) collective-permute-start(bf16[64,2048]{1,0:T(8,128)(2,1)S(1)} %add_convert_fusion.refs_0_), channel_id=1, source_target_pairs={{0,256},{128,384},{256,0},{384,128},{1,257},{129,385},{257,1},{385... | collective-permute-start | bytes 786440 | tf_op jit(solution)/shard_map/ppermute | solution.py:142
  54.4 12.2 %collective-permute-start.2 = (bf16[64,2048]{1,0:T(8,128)(2,1)S(1)}, bf16[64,2048]{1,0:T(8,128)(2,1)S(1)}, u32[]{:S(2)}, u32[]{:S(2)}) collective-permute-start(bf16[64,2048]{1,0:T(8,128)(2,1)S(1)} %add_convert_fusion.refs_0_), channel_id=1, source_target_pairs={{0,128},{128,0},{256,384},{384,256},{1,129},{129,1},{257,385},{385... | collective-permute-start | bytes 786440 | tf_op jit(solution)/shard_map/ppermute | solution.py:142
  61.4 6.4 %collective-permute-start.4 = (bf16[64,2048]{1,0:T(8,128)(2,1)S(1)}, bf16[64,2048]{1,0:T(8,128)(2,1)S(1)}, u32[]{:S(2)}, u32[]{:S(2)}) collective-permute-start(bf16[64,2048]{1,0:T(8,128)(2,1)S(1)} %collective-permute-done.3.refs_2_), channel_id=1, source_target_pairs={{0,128},{128,0},{256,384},{384,256},{1,129},{129,1},{257,385},{385... | collective-permute-start | bytes 786440 | tf_op jit(solution)/shard_map/ppermute | solution.py:142
  67.7 1.4 %copy-start.1 = (f32[32,1,2,2048]{3,2,1,0:T(2,128)S(1)}, f32[32,1,2,2048]{3,2,1,0:T(2,128)}, u32[]{:S(2)}) copy-start(f32[32,1,2,2048]{3,2,1,0:T(2,128)} %param.4) | copy-start | bytes 1572868
  67.7 1.4 %copy-start.2 = (f32[32,1,2,2048]{3,2,1,0:T(2,128)S(1)}, f32[32,1,2,2048]{3,2,1,0:T(2,128)}, u32[]{:S(2)}) copy-start(f32[32,1,2,2048]{3,2,1,0:T(2,128)} %param.5) | copy-start | bytes 1572868

commit v5 on v4

--- a/solution.py
+++ b/solution.py
@@ -9,8 +9,8 @@
 BF16 = jnp.bfloat16
 VMEM = pl.BlockSpec(memory_space=pltpu.VMEM)
 SMEM = pl.BlockSpec(memory_space=pltpu.SMEM)
-ANY = pl.BlockSpec(memory_space=pl.ANY)
-PARAMS = pltpu.CompilerParams(vmem_limit_bytes=32 * 1024 * 1024)
+HBM = pl.BlockSpec(memory_space=pltpu.HBM)
+PARAMS = pltpu.CompilerParams(vmem_limit_bytes=16 * 1024 * 1024)
 FIRST = 11
 
 
@@ -27,18 +27,20 @@
 
 
 def first_kernel(chip_ref, weights_ref, momentum_ref, parts_ref, state_ref, other_ref, *scratch):
-    weights, momentum, state, sems = scratch
-    other = pltpu.make_async_copy(parts_ref.at[1 - chip_ref[0]], other_ref, sems.at[3, 0])
-    runs = list(segments(weights.shape[0]))
-    loads, stores = [], []
+    weights, momentum, state, other, sems = scratch
+    runs = sorted(segments(weights.shape[0]), key=lambda run: -run[2])
+    take = pltpu.make_async_copy(parts_ref.at[1 - chip_ref[0]], other, sems.at[3, 0])
+    give = pltpu.make_async_copy(other, other_ref, sems.at[3, 1])
+    take.start()
+    loads, stores = [], [give]
     for n, (place, index, length) in enumerate(runs):
         rows = pl.ds(index, length)
         for m, (source, target) in enumerate(((weights_ref, weights), (momentum_ref, momentum))):
             copy = pltpu.make_async_copy(source.at[rows], target.at[rows], sems.at[m, n])
             copy.start()
             loads.append(copy)
-        if n == 0:
-            other.start()
+    take.wait()
+    give.start()
     for n, (place, index, length) in enumerate(runs):
         loads[2 * n].wait()
         loads[2 * n + 1].wait()
@@ -47,7 +49,6 @@
         copy = pltpu.make_async_copy(state.at[places], state_ref.at[places], sems.at[2, n])
         copy.start()
         stores.append(copy)
-    other.wait()
     for copy in stores:
         copy.wait()
 
@@ -56,8 +57,8 @@
     shape = weights.shape
     return pl.pallas_call(
         first_kernel,
-        in_specs=[SMEM, ANY, ANY, ANY],
-        out_specs=[ANY, VMEM],
+        in_specs=[SMEM, HBM, HBM, HBM],
+        out_specs=[HBM, HBM],
         out_shape=[
             jax.ShapeDtypeStruct(shape, BF16),
             jax.ShapeDtypeStruct(parts.shape[1:], BF16),
@@ -66,52 +67,120 @@
             pltpu.VMEM(shape, F32),
             pltpu.VMEM(shape, F32),
             pltpu.VMEM(shape, BF16),
+            pltpu.VMEM(parts.shape[1:], BF16),
             pltpu.SemaphoreType.DMA((4, 4)),
         ],
         cost_estimate=cost(3 << 20),
     )(chip.reshape(1), weights, momentum, parts)
 
 
-def update_kernel(total_ref, weights_ref, momentum_ref, outer_ref, out_momentum_ref):
-    for place, index, length in segments(weights_ref.shape[0]):
+def update_kernel(total_ref, weights_ref, momentum_ref, outer_ref, out_momentum_ref, outer, out_momentum, sems):
+    stores = []
+    for n, (place, index, length) in enumerate(segments(weights_ref.shape[0])):
         rows = pl.ds(index, length)
         weights = weights_ref[rows]
         pseudo_grad = weights - 0.25 * total_ref[pl.ds(place, length)].astype(F32)
         momentum = 0.9 * momentum_ref[rows] + pseudo_grad
-        out_momentum_ref[rows] = momentum
-        outer_ref[rows] = weights - 0.7 * (pseudo_grad + 0.9 * momentum)
+        out_momentum[rows] = momentum
+        outer[rows] = weights - 0.7 * (pseudo_grad + 0.9 * momentum)
+        for m, (value, ref) in enumerate(((outer, outer_ref), (out_momentum, out_momentum_ref))):
+            copy = pltpu.make_async_copy(value.at[rows], ref.at[rows], sems.at[m, n])
+            copy.start()
+            stores.append(copy)
+    for copy in stores:
+        copy.wait()
 
 
 def update(total, weights, momentum):
     return pl.pallas_call(
         update_kernel,
         in_specs=[VMEM] * 3,
-        out_specs=[VMEM] * 2,
+        out_specs=[HBM] * 2,
         out_shape=[jax.ShapeDtypeStruct(weights.shape, F32)] * 2,
+        scratch_shapes=[
+            pltpu.VMEM(weights.shape, F32),
+            pltpu.VMEM(weights.shape, F32),
+            pltpu.SemaphoreType.DMA((2, 4)),
+        ],
         cost_estimate=cost(3 << 20),
         compiler_params=PARAMS,
     )(total, weights, momentum)
 
 
+def mixed_rows(shard, copy):
+    return (0.5 * shard.astype(F32) + 0.5 * copy.astype(F32)).astype(BF16)
+
+
+def rows_of(place, quarter):
+    return pl.ds(pl.multiple_of(place * quarter, quarter), quarter)
+
+
 def mix_kernel(rep_ref, shard_ref, *refs):
-    *copy_refs, out_ref = refs
+    *copy_refs, out_ref, rest_ref, shard, out, sems = refs
     rep = rep_ref[0]
-    quarter = copy_refs[0].shape[0]
+    quarter = rest_ref.shape[0]
+    last = len(copy_refs)
+    rows = [rows_of(rep ^ i, quarter) for i in range(last + 1)]
+    loads = [
+        pltpu.make_async_copy(shard_ref.at[rows[i]], shard.at[i], sems.at[0, i])
+        for i in range(last)
+    ]
+    loads.append(pltpu.make_async_copy(shard_ref.at[rows[last]], rest_ref, sems.at[0, last]))
+    stores = [
+        pltpu.make_async_copy(out.at[i], out_ref.at[rows[i]], sems.at[1, i]) for i in range(last)
+    ]
+    for load in loads:
+        load.start()
     for i, copy_ref in enumerate(copy_refs):
-        rows = pl.ds(pl.multiple_of((rep ^ i) * quarter, quarter), quarter)
-        value = 0.5 * shard_ref[rows, :].astype(F32) + 0.5 * copy_ref[...].astype(F32)
-        out_ref[rows, :] = value.astype(BF16)
+        loads[i].wait()
+        out[i] = mixed_rows(shard[i], copy_ref[...])
+        stores[i].start()
+    loads[last].wait()
+    for store in stores:
+        store.wait()
 
 
 def mix(rep, shard, copies):
+    quarter = copies[0].shape
+    count = len(copies)
     return pl.pallas_call(
         mix_kernel,
-        in_specs=[SMEM] + [VMEM] * (1 + len(copies)),
-        out_specs=VMEM,
-        out_shape=jax.ShapeDtypeStruct(shard.shape, BF16),
-        cost_estimate=cost(3 << 20),
+        in_specs=[SMEM, HBM] + [VMEM] * count,
+        out_specs=[HBM, VMEM],
+        out_shape=[
+            jax.ShapeDtypeStruct(shard.shape, BF16),
+            jax.ShapeDtypeStruct(quarter, BF16),
+        ],
+        scratch_shapes=[
+            pltpu.VMEM((count, *quarter), BF16),
+            pltpu.VMEM((count, *quarter), BF16),
+            pltpu.SemaphoreType.DMA((2, count + 1)),
+        ],
+        cost_estimate=cost(3 << 19),
         compiler_params=PARAMS,
     )(rep.reshape(1), shard, *copies)
+
+
+def rest_kernel(place_ref, shard_ref, copy_ref, before_ref, out_ref, out, sem):
+    del before_ref
+    out[...] = mixed_rows(shard_ref[...], copy_ref[...])
+    rows = rows_of(place_ref[0], out.shape[0])
+    store = pltpu.make_async_copy(out, out_ref.at[rows], sem)
+    store.start()
+    store.wait()
+
+
+def mix_rest(place, shard, copy, before):
+    return pl.pallas_call(
+        rest_kernel,
+        in_specs=[SMEM, VMEM, VMEM, HBM],
+        out_specs=HBM,
+        out_shape=jax.ShapeDtypeStruct(before.shape, BF16),
+        scratch_shapes=[pltpu.VMEM(copy.shape, BF16), pltpu.SemaphoreType.DMA],
+        input_output_aliases={3: 0},
+        cost_estimate=cost(3 << 18),
+        compiler_params=PARAMS,
+    )(place.reshape(1), shard, copy, before)
 
 
 def on_device(inner_weights, outer_weights, outer_momentum):
@@ -159,7 +228,8 @@
     beside = swap(copy, 1)
     across = swap(copy, 2)
     diagonal = swap(across, 1)
-    mixed = mix(rep, shard, [copy, beside, across, diagonal])
+    mixed, rest = mix(rep, shard, [copy, beside, across])
+    mixed = mix_rest(rep ^ 3, rest, diagonal, mixed)
 
     new_outer, new_momentum = update(inner_total, outer_here, momentum_here)
     return (mixed[None], new_outer[:, None], new_momentum[:, None])

time: 70.6 us -> 69.8 us (0.989)
  waiting for transfers between devices: 12 us -> 9.92 us
  other arithmetic: 1.58 us -> 2.53 us
    all_to_all x2, waiting for transfers between devices: 7.77 us -> 6.7 us  [exchange(): lax.all_to_all(value, 'fsdp', split_axis=0, concat_axis=0, axis_index_gro...]
    ppermute x5, waiting for transfers between devices: 4.22 us -> 3.23 us  [swap(): return lax.ppermute(value, 'rep', [(r, r ^ i) for r in range(replicas)])]
    convert_element_type x1, other arithmetic: 0.06 us -> 1.01 us  [on_device(): sent = turn(total.astype(BF16).reshape(blocks, group, columns), FIRST)]
    pallas_call x3 -> x4, Pallas kernels: 5.59 us -> 5.29 us  [the longest x1 2.28 us: state_and_other(): pl.pallas_call(first_kernel, in_specs=[SMEM, HBM, HBM, HBM], out_specs=[H...]
  transfers between devices with their start and end apart: 7 -> 7, of which waited for: 4 -> 3; matrix products, arithmetic and copies ran while one was open for 4% -> 5% of each run, Pallas kernels for 2% -> 3%
where the time goes in v5:
time: 69.8 us; the launch traced here: 69.3 us
  starting transfers between devices  49.2 us (70%)
  waiting for transfers between devices  9.92 us (14%)
  Pallas kernels  5.29 us (8%)
  other arithmetic  2.53 us (4%)
  local copies, waits for them, and re-layouts  1.41 us (2%)
  between operations  0.91 us (1%)
    all_to_all x2, starting transfers between devices, exchange(): lax.all_to_all(value, 'fsdp', split_axis=0, concat_axis=0, axis_index_gro...  29.7 us
    ppermute x5, starting transfers between devices, swap(): return lax.ppermute(value, 'rep', [(r, r ^ i) for r in range(replicas)])  19.5 us
    all_to_all x2, waiting for transfers between devices, exchange(): lax.all_to_all(value, 'fsdp', split_axis=0, concat_axis=0, axis_index_gro...  6.7 us
    ppermute x5, waiting for transfers between devices, swap(): return lax.ppermute(value, 'rep', [(r, r ^ i) for r in range(replicas)])  3.23 us
    pallas_call x1, Pallas kernels, state_and_other(): pl.pallas_call(first_kernel, in_specs=[SMEM, HBM, HBM, HBM], out_specs=[H...  2.28 us
  transfers between devices with their start and end apart: 7, of which 3 were waited for; matrix products, arithmetic and copies ran while one was open for 5% of the time, Pallas kernels for 3%

profile of v5, /device:TPU:1, one launch (start us, length us, event | category | flops | bytes accessed | tf_op | source)
XLA Modules:
  0.0 69.3 jit_solution(10309751130710590103)
XLA Ops:
  0.6 0.0 copy-start
  0.7 2.3 %shard_map.58 = (bf16[32,2,2048]{2,1,0:T(2,128)(2,1)}, bf16[128,2048]{1,0:T(8,128)(2,1)}) custom-call(s32[1]{0:T(128)} %bitcast.3.chip_ref, f32[32,2,2048]{2,1,0:T(2,128)} %bitcast.28, f32[32,2,2048]{2,1,0:T(2,128)} %bitcast.30, bf16[2,128,2048]{2,1,0:T(8,128)(2,1)} %bitcast.25), custom_call_target="tpu_custom_call" | custom-call | bytes 3145728 | tf_op jit(solution)/shard_map/pallas_call | solution.py:58
  2.9 3.9 %collective-permute-start = (bf16[128,2048]{1,0:T(8,128)(2,1)}, bf16[128,2048]{1,0:T(8,128)(2,1)S(1)}, u32[]{:S(2)}, u32[]{:S(2)}) collective-permute-start(bf16[128,2048]{1,0:T(8,128)(2,1)} %get-tuple-element.12), channel_id=1, source_target_pairs={{0,256},{128,384},{256,0},{384,128},{1,257},{129,385},{257,1},{385... | collective-permute-start | bytes 1572872 | tf_op jit(solution)/shard_map/ppermute | solution.py:211
  6.9 17.9 %all-to-all-start = ((bf16[32,2,2048]{2,1,0:T(2,128)(2,1)}), bf16[32,2,2048]{2,1,0:T(2,128)(2,1)S(1)}, u32[]{:S(2)}, u32[]{:S(2)}) async-start(bf16[32,2,2048]{2,1,0:T(2,128)(2,1)} %get-tuple-element.11), calls=%async_computation | async-start | bytes 524288 | tf_op jit(solution)/shard_map/all_to_all | solution.py:201
  24.8 0.0 collective-permute-done
  24.9 0.0 copy-done
  24.9 0.1 convert_add_fusion
  25.0 3.4 %collective-permute-start.1 = (bf16[64,2048]{1,0:T(8,128)(2,1)S(1)}, bf16[64,2048]{1,0:T(8,128)(2,1)}, u32[]{:S(2)}, u32[]{:S(2)}) collective-permute-start(bf16[64,2048]{1,0:T(8,128)(2,1)S(1)} %fusion), channel_id=1, source_target_pairs={{0,128},{128,0},{256,384},{384,256},{1,129},{129,1},{257,385},{385... | collective-permute-start | bytes 786440 | tf_op jit(solution)/shard_map/ppermute | solution.py:211
  28.5 1.3 %collective-permute-done.1 = bf16[64,2048]{1,0:T(8,128)(2,1)} collective-permute-done((bf16[64,2048]{1,0:T(8,128)(2,1)S(1)}, bf16[64,2048]{1,0:T(8,128)(2,1)}, u32[]{:S(2)}, u32[]{:S(2)}) %collective-permute-start.1) | collective-permute-done | bytes 262176 | tf_op jit(solution)/shard_map/ppermute | solution.py:211
  29.7 1.0 %fusion.1 = (bf16[64,2048]{1,0:T(8,128)(2,1)S(1)}, f32[64,2048]{1,0:T(8,128)S(1)}) fusion(bf16[64,2048]{1,0:T(8,128)(2,1)} %collective-permute-done.1, f32[2,64,2048]{2,1,0:T(8,128)S(1)} %bitcast.33, s32[]{:T(128)S(6)} %select_n.25), kind=kLoop, calls=%fused_computation.7 | loop fusion | flops 393216 | bytes 1572868 | tf_op jit(solution)/shard_map/convert_element_type | solution.py:223
  30.8 0.2 reshape_reshape.4
  31.0 0.1 slice.18
  31.0 0.1 slice.19
  31.2 1.0 %pad_maximum_fusion = bf16[2,16,2,2048]{3,2,1,0:T(2,128)(2,1)} fusion(bf16[2,11,2,2048]{3,2,1,0:T(2,128)(2,1)S(1)} %slice.19, bf16[2,5,2,2048]{3,2,1,0:T(2,128)(2,1)S(1)} %slice.18), kind=kLoop, calls=%fused_computation.6 | loop fusion | flops 131072 | bytes 524288 | tf_op jit(solution)/shard_map/concatenate | solution.py:207
  32.2 6.7 %all-to-all-done = bf16[32,2,2048]{2,1,0:T(2,128)(2,1)S(1)} async-done(((bf16[32,2,2048]{2,1,0:T(2,128)(2,1)}), bf16[32,2,2048]{2,1,0:T(2,128)(2,1)S(1)}, u32[]{:S(2)}, u32[]{:S(2)}) %all-to-all-start) | async-done | bytes 262176 | tf_op jit(solution)/shard_map/all_to_all | solution.py:201
  38.9 11.8 %all-to-all-start.1 = ((bf16[32,2,2048]{2,1,0:T(2,128)(2,1)}), bf16[32,2,2048]{2,1,0:T(2,128)(2,1)S(1)}, u32[]{:S(2)}, u32[]{:S(2)}) async-start(bf16[32,2,2048]{2,1,0:T(2,128)(2,1)} %bitcast.12), calls=%async_computation.1 | async-start | bytes 524288 | tf_op jit(solution)/shard_map/all_to_all | solution.py:201
  50.7 0.1 slice.17
  50.8 0.1 slice.16
  50.9 0.3 maximum_convert_fusion
  51.2 0.4 reshape.35
  51.6 0.1 add_convert_fusion.refs_0_
  51.6 1.9 %collective-permute-start.3 = (bf16[64,2048]{1,0:T(8,128)(2,1)S(1)}, bf16[64,2048]{1,0:T(8,128)(2,1)S(1)}, u32[]{:S(2)}, u32[]{:S(2)}) collective-permute-start(bf16[64,2048]{1,0:T(8,128)(2,1)S(1)} %add_convert_fusion.refs_0_), channel_id=1, source_target_pairs={{0,256},{128,384},{256,0},{384,128},{1,257},{129,385},{257,1},{385... | collective-permute-start | bytes 786440 | tf_op jit(solution)/shard_map/ppermute | solution.py:211
  53.5 5.0 %collective-permute-start.2 = (bf16[64,2048]{1,0:T(8,128)(2,1)S(1)}, bf16[64,2048]{1,0:T(8,128)(2,1)S(1)}, u32[]{:S(2)}, u32[]{:S(2)}) collective-permute-start(bf16[64,2048]{1,0:T(8,128)(2,1)S(1)} %add_convert_fusion.refs_0_), channel_id=1, source_target_pairs={{0,128},{128,0},{256,384},{384,256},{1,129},{129,1},{257,385},{385... | collective-permute-start | bytes 786440 | tf_op jit(solution)/shard_map/ppermute | solution.py:211
  58.6 2.0 %collective-permute-done.3.refs_2_ = bf16[64,2048]{1,0:T(8,128)(2,1)S(1)} collective-permute-done((bf16[64,2048]{1,0:T(8,128)(2,1)S(1)}, bf16[64,2048]{1,0:T(8,128)(2,1)S(1)}, u32[]{:S(2)}, u32[]{:S(2)}) %collective-permute-start.3) | collective-permute-done | bytes 262176 | tf_op jit(solution)/shard_map/ppermute | solution.py:211
  60.5 5.2 %collective-permute-start.4 = (bf16[64,2048]{1,0:T(8,128)(2,1)S(1)}, bf16[64,2048]{1,0:T(8,128)(2,1)S(1)}, u32[]{:S(2)}, u32[]{:S(2)}) collective-permute-start(bf16[64,2048]{1,0:T(8,128)(2,1)S(1)} %collective-permute-done.3.refs_2_), channel_id=1, source_target_pairs={{0,128},{128,0},{256,384},{384,256},{1,129},{129,1},{257,385},{385... | collective-permute-start | bytes 786440 | tf_op jit(solution)/shard_map/ppermute | solution.py:211
  65.8 0.0 collective-permute-done.2.refs_1_
  65.8 1.1 %shard_map.59 = (bf16[256,2048]{1,0:T(8,128)(2,1)}, bf16[64,2048]{1,0:T(8,128)(2,1)S(1)}) custom-call(s32[1]{0:T(128)} %bitcast.1.rep_ref, bf16[256,2048]{1,0:T(8,128)(2,1)S(1)} %bitcast.27, bf16[64,2048]{1,0:T(8,128)(2,1)S(1)} %add_convert_fusion.refs_0_, bf16[64,2048]{1,0:T(8,128)(2,1)S(1)} %collective-permute-done.2.refs_1_, ...), custom_call_target="tpu_custom_call" | custom-call | bytes 1572864 | tf_op jit(solution)/shard_map/pallas_call | solution.py:146
  66.9 0.0 collective-permute-done.4.copy_ref
  66.9 0.0 copy-start.1
  67.0 0.0 copy-start.2
  67.0 0.8 %shard_map.60 = bf16[256,2048]{1,0:T(8,128)(2,1)} custom-call(s32[1]{0:T(128)} %bitcast.place_ref, bf16[64,2048]{1,0:T(8,128)(2,1)S(1)} %get-tuple-element.14.shard_ref, bf16[64,2048]{1,0:T(8,128)(2,1)S(1)} %collective-permute-done.4.copy_ref, bf16[256,2048]{1,0:T(8,128)(2,1)} %get-tuple-element.15.before_ref), custom_call_target="tpu_custom_call", output_to_operand_aliasing={{}: (3, {})} | custom-call | bytes 786432 | tf_op jit(solution)/shard_map/pallas_call | solution.py:174
  67.8 0.0 all-to-all-done.1.total_ref
  67.8 0.2 copy-done.1
  68.0 0.2 copy-done.2
  68.2 1.1 %shard_map.61 = (f32[32,2,2048]{2,1,0:T(2,128)}, f32[32,2,2048]{2,1,0:T(2,128)}) custom-call(bf16[32,2,2048]{2,1,0:T(2,128)(2,1)S(1)} %all-to-all-done.1.total_ref, f32[32,2,2048]{2,1,0:T(2,128)S(1)} %bitcast.29, f32[32,2,2048]{2,1,0:T(2,128)S(1)} %bitcast.31), custom_call_target="tpu_custom_call" | custom-call | bytes 3145728 | tf_op jit(solution)/shard_map/pallas_call | solution.py:95
  (1 shorter events, 0.0 us)
Async XLA Ops:
  0.6 24.2 %copy-start = (bf16[1,256,2048]{2,1,0:T(8,128)(2,1)S(1)}, bf16[1,256,2048]{2,1,0:T(8,128)(2,1)}, u32[]{:S(2)}) copy-start(bf16[1,256,2048]{2,1,0:T(8,128)(2,1)} %param.3) | copy-start | bytes 3145732
  2.9 21.9 %collective-permute-start = (bf16[128,2048]{1,0:T(8,128)(2,1)}, bf16[128,2048]{1,0:T(8,128)(2,1)S(1)}, u32[]{:S(2)}, u32[]{:S(2)}) collective-permute-start(bf16[128,2048]{1,0:T(8,128)(2,1)} %get-tuple-element.12), channel_id=1, source_target_pairs={{0,256},{128,384},{256,0},{384,128},{1,257},{129,385},{257,1},{385... | collective-permute-start | bytes 1572872 | tf_op jit(solution)/shard_map/ppermute | solution.py:211
  6.9 32.0 %all-to-all-start = ((bf16[32,2,2048]{2,1,0:T(2,128)(2,1)}), bf16[32,2,2048]{2,1,0:T(2,128)(2,1)S(1)}, u32[]{:S(2)}, u32[]{:S(2)}) async-start(bf16[32,2,2048]{2,1,0:T(2,128)(2,1)} %get-tuple-element.11), calls=%async_computation | async-start | bytes 524288 | tf_op jit(solution)/shard_map/all_to_all | solution.py:201
  25.0 4.7 %collective-permute-start.1 = (bf16[64,2048]{1,0:T(8,128)(2,1)S(1)}, bf16[64,2048]{1,0:T(8,128)(2,1)}, u32[]{:S(2)}, u32[]{:S(2)}) collective-permute-start(bf16[64,2048]{1,0:T(8,128)(2,1)S(1)} %fusion), channel_id=1, source_target_pairs={{0,128},{128,0},{256,384},{384,256},{1,129},{129,1},{257,385},{385... | collective-permute-start | bytes 786440 | tf_op jit(solution)/shard_map/ppermute | solution.py:211
  38.9 28.9 %all-to-all-start.1 = ((bf16[32,2,2048]{2,1,0:T(2,128)(2,1)}), bf16[32,2,2048]{2,1,0:T(2,128)(2,1)S(1)}, u32[]{:S(2)}, u32[]{:S(2)}) async-start(bf16[32,2,2048]{2,1,0:T(2,128)(2,1)} %bitcast.12), calls=%async_computation.1 | async-start | bytes 524288 | tf_op jit(solution)/shard_map/all_to_all | solution.py:201
  51.6 8.9 %collective-permute-start.3 = (bf16[64,2048]{1,0:T(8,128)(2,1)S(1)}, bf16[64,2048]{1,0:T(8,128)(2,1)S(1)}, u32[]{:S(2)}, u32[]{:S(2)}) collective-permute-start(bf16[64,2048]{1,0:T(8,128)(2,1)S(1)} %add_convert_fusion.refs_0_), channel_id=1, source_target_pairs={{0,256},{128,384},{256,0},{384,128},{1,257},{129,385},{257,1},{385... | collective-permute-start | bytes 786440 | tf_op jit(solution)/shard_map/ppermute | solution.py:211
  53.5 12.2 %collective-permute-start.2 = (bf16[64,2048]{1,0:T(8,128)(2,1)S(1)}, bf16[64,2048]{1,0:T(8,128)(2,1)S(1)}, u32[]{:S(2)}, u32[]{:S(2)}) collective-permute-start(bf16[64,2048]{1,0:T(8,128)(2,1)S(1)} %add_convert_fusion.refs_0_), channel_id=1, source_target_pairs={{0,128},{128,0},{256,384},{384,256},{1,129},{129,1},{257,385},{385... | collective-permute-start | bytes 786440 | tf_op jit(solution)/shard_map/ppermute | solution.py:211
  60.5 6.4 %collective-permute-start.4 = (bf16[64,2048]{1,0:T(8,128)(2,1)S(1)}, bf16[64,2048]{1,0:T(8,128)(2,1)S(1)}, u32[]{:S(2)}, u32[]{:S(2)}) collective-permute-start(bf16[64,2048]{1,0:T(8,128)(2,1)S(1)} %collective-permute-done.3.refs_2_), channel_id=1, source_target_pairs={{0,128},{128,0},{256,384},{384,256},{1,129},{129,1},{257,385},{385... | collective-permute-start | bytes 786440 | tf_op jit(solution)/shard_map/ppermute | solution.py:211
  66.9 1.1 %copy-start.1 = (f32[32,1,2,2048]{3,2,1,0:T(2,128)S(1)}, f32[32,1,2,2048]{3,2,1,0:T(2,128)}, u32[]{:S(2)}) copy-start(f32[32,1,2,2048]{3,2,1,0:T(2,128)} %param.4) | copy-start | bytes 1572868
  67.0 1.3 %copy-start.2 = (f32[32,1,2,2048]{3,2,1,0:T(2,128)S(1)}, f32[32,1,2,2048]{3,2,1,0:T(2,128)}, u32[]{:S(2)}) copy-start(f32[32,1,2,2048]{3,2,1,0:T(2,128)} %param.5) | copy-start | bytes 1572868

commit v6 on v5

--- a/solution.py
+++ b/solution.py
@@ -10,7 +10,7 @@
 VMEM = pl.BlockSpec(memory_space=pltpu.VMEM)
 SMEM = pl.BlockSpec(memory_space=pltpu.SMEM)
 HBM = pl.BlockSpec(memory_space=pltpu.HBM)
-PARAMS = pltpu.CompilerParams(vmem_limit_bytes=16 * 1024 * 1024)
+PARAMS = pltpu.CompilerParams(vmem_limit_bytes=8 * 1024 * 1024)
 FIRST = 11
 
 
@@ -28,19 +28,29 @@
 
 def first_kernel(chip_ref, weights_ref, momentum_ref, parts_ref, state_ref, other_ref, *scratch):
     weights, momentum, state, other, sems = scratch
-    runs = sorted(segments(weights.shape[0]), key=lambda run: -run[2])
-    take = pltpu.make_async_copy(parts_ref.at[1 - chip_ref[0]], other, sems.at[3, 0])
-    give = pltpu.make_async_copy(other, other_ref, sems.at[3, 1])
-    take.start()
-    loads, stores = [], [give]
+    runs = []
+    for place, index, length in segments(weights.shape[0]):
+        half = length // 2
+        runs += [(place, index, half), (place + half, index + half, length - half)]
+    runs.sort(key=lambda run: -run[2])
+    takes, gives = [], []
+    quarter = other.shape[0] // 4
+    for n in range(4):
+        rows = pl.ds(n * quarter, quarter)
+        source = parts_ref.at[1 - chip_ref[0], rows]
+        takes.append(pltpu.make_async_copy(source, other.at[rows], sems.at[3, n]))
+        gives.append(pltpu.make_async_copy(other.at[rows], other_ref.at[rows], sems.at[3, 4 + n]))
+        takes[n].start()
+    loads, stores = [], []
     for n, (place, index, length) in enumerate(runs):
         rows = pl.ds(index, length)
         for m, (source, target) in enumerate(((weights_ref, weights), (momentum_ref, momentum))):
             copy = pltpu.make_async_copy(source.at[rows], target.at[rows], sems.at[m, n])
             copy.start()
             loads.append(copy)
-    take.wait()
-    give.start()
+    for take, give in zip(takes, gives):
+        take.wait()
+        give.start()
     for n, (place, index, length) in enumerate(runs):
         loads[2 * n].wait()
         loads[2 * n + 1].wait()
@@ -49,7 +59,7 @@
         copy = pltpu.make_async_copy(state.at[places], state_ref.at[places], sems.at[2, n])
         copy.start()
         stores.append(copy)
-    for copy in stores:
+    for copy in gives + stores:
         copy.wait()
 
 
@@ -68,7 +78,7 @@
             pltpu.VMEM(shape, F32),
             pltpu.VMEM(shape, BF16),
             pltpu.VMEM(parts.shape[1:], BF16),
-            pltpu.SemaphoreType.DMA((4, 4)),
+            pltpu.SemaphoreType.DMA((4, 8)),
         ],
         cost_estimate=cost(3 << 20),
     )(chip.reshape(1), weights, momentum, parts)
@@ -156,7 +166,7 @@
             pltpu.VMEM((count, *quarter), BF16),
             pltpu.SemaphoreType.DMA((2, count + 1)),
         ],
-        cost_estimate=cost(3 << 19),
+        cost_estimate=cost(1 << 17),
         compiler_params=PARAMS,
     )(rep.reshape(1), shard, *copies)
 
@@ -178,7 +188,7 @@
         out_shape=jax.ShapeDtypeStruct(before.shape, BF16),
         scratch_shapes=[pltpu.VMEM(copy.shape, BF16), pltpu.SemaphoreType.DMA],
         input_output_aliases={3: 0},
-        cost_estimate=cost(3 << 18),
+        cost_estimate=cost(1 << 16),
         compiler_params=PARAMS,
     )(place.reshape(1), shard, copy, before)
 

time: 69.8 us -> 70 us (level)
  no operation moved by 1% of the time
where the time goes in v6:
time: 70 us; the launch traced here: 69.5 us
  starting transfers between devices  49.2 us (70%)
  waiting for transfers between devices  9.92 us (14%)
  Pallas kernels  5.49 us (8%)
  other arithmetic  2.53 us (4%)
  local copies, waits for them, and re-layouts  1.41 us (2%)
  between operations  0.91 us (1%)
    all_to_all x2, starting transfers between devices, exchange(): lax.all_to_all(value, 'fsdp', split_axis=0, concat_axis=0, axis_index_gro...  29.7 us
    ppermute x5, starting transfers between devices, swap(): return lax.ppermute(value, 'rep', [(r, r ^ i) for r in range(replicas)])  19.5 us
    all_to_all x2, waiting for transfers between devices, exchange(): lax.all_to_all(value, 'fsdp', split_axis=0, concat_axis=0, axis_index_gro...  6.7 us
    ppermute x5, waiting for transfers between devices, swap(): return lax.ppermute(value, 'rep', [(r, r ^ i) for r in range(replicas)])  3.23 us
    pallas_call x1, Pallas kernels, state_and_other(): pl.pallas_call(first_kernel, in_specs=[SMEM, HBM, HBM, HBM], out_specs=[H...  2.48 us
  transfers between devices with their start and end apart: 7, of which 3 were waited for; matrix products, arithmetic and copies ran while one was open for 5% of the time, Pallas kernels for 3%

profile of v6, /device:TPU:1, one launch (start us, length us, event | category | flops | bytes accessed | tf_op | source)
XLA Modules:
  0.0 69.5 jit_solution(9714652193639974117)
XLA Ops:
  0.6 0.0 copy-start
  0.7 2.5 %shard_map.58 = (bf16[32,2,2048]{2,1,0:T(2,128)(2,1)}, bf16[128,2048]{1,0:T(8,128)(2,1)}) custom-call(s32[1]{0:T(128)} %bitcast.3.chip_ref, f32[32,2,2048]{2,1,0:T(2,128)} %bitcast.28, f32[32,2,2048]{2,1,0:T(2,128)} %bitcast.30, bf16[2,128,2048]{2,1,0:T(8,128)(2,1)} %bitcast.25), custom_call_target="tpu_custom_call" | custom-call | bytes 3145728 | tf_op jit(solution)/shard_map/pallas_call | solution.py:68
  3.1 3.9 %collective-permute-start = (bf16[128,2048]{1,0:T(8,128)(2,1)}, bf16[128,2048]{1,0:T(8,128)(2,1)S(1)}, u32[]{:S(2)}, u32[]{:S(2)}) collective-permute-start(bf16[128,2048]{1,0:T(8,128)(2,1)} %get-tuple-element.12), channel_id=1, source_target_pairs={{0,256},{128,384},{256,0},{384,128},{1,257},{129,385},{257,1},{385... | collective-permute-start | bytes 1572872 | tf_op jit(solution)/shard_map/ppermute | solution.py:221
  7.1 17.9 %all-to-all-start = ((bf16[32,2,2048]{2,1,0:T(2,128)(2,1)}), bf16[32,2,2048]{2,1,0:T(2,128)(2,1)S(1)}, u32[]{:S(2)}, u32[]{:S(2)}) async-start(bf16[32,2,2048]{2,1,0:T(2,128)(2,1)} %get-tuple-element.11), calls=%async_computation | async-start | bytes 524288 | tf_op jit(solution)/shard_map/all_to_all | solution.py:211
  25.0 0.0 collective-permute-done
  25.1 0.0 copy-done
  25.1 0.1 convert_add_fusion
  25.2 3.4 %collective-permute-start.1 = (bf16[64,2048]{1,0:T(8,128)(2,1)S(1)}, bf16[64,2048]{1,0:T(8,128)(2,1)}, u32[]{:S(2)}, u32[]{:S(2)}) collective-permute-start(bf16[64,2048]{1,0:T(8,128)(2,1)S(1)} %fusion), channel_id=1, source_target_pairs={{0,128},{128,0},{256,384},{384,256},{1,129},{129,1},{257,385},{385... | collective-permute-start | bytes 786440 | tf_op jit(solution)/shard_map/ppermute | solution.py:221
  28.7 1.3 %collective-permute-done.1 = bf16[64,2048]{1,0:T(8,128)(2,1)} collective-permute-done((bf16[64,2048]{1,0:T(8,128)(2,1)S(1)}, bf16[64,2048]{1,0:T(8,128)(2,1)}, u32[]{:S(2)}, u32[]{:S(2)}) %collective-permute-start.1) | collective-permute-done | bytes 262176 | tf_op jit(solution)/shard_map/ppermute | solution.py:221
  29.9 1.0 %fusion.1 = (bf16[64,2048]{1,0:T(8,128)(2,1)S(1)}, f32[64,2048]{1,0:T(8,128)S(1)}) fusion(bf16[64,2048]{1,0:T(8,128)(2,1)} %collective-permute-done.1, f32[2,64,2048]{2,1,0:T(8,128)S(1)} %bitcast.33, s32[]{:T(128)S(6)} %select_n.25), kind=kLoop, calls=%fused_computation.7 | loop fusion | flops 393216 | bytes 1572868 | tf_op jit(solution)/shard_map/convert_element_type | solution.py:233
  31.0 0.2 reshape_reshape.4
  31.2 0.1 slice.18
  31.2 0.1 slice.19
  31.4 1.0 %pad_maximum_fusion = bf16[2,16,2,2048]{3,2,1,0:T(2,128)(2,1)} fusion(bf16[2,11,2,2048]{3,2,1,0:T(2,128)(2,1)S(1)} %slice.19, bf16[2,5,2,2048]{3,2,1,0:T(2,128)(2,1)S(1)} %slice.18), kind=kLoop, calls=%fused_computation.6 | loop fusion | flops 131072 | bytes 524288 | tf_op jit(solution)/shard_map/concatenate | solution.py:217
  32.4 6.7 %all-to-all-done = bf16[32,2,2048]{2,1,0:T(2,128)(2,1)S(1)} async-done(((bf16[32,2,2048]{2,1,0:T(2,128)(2,1)}), bf16[32,2,2048]{2,1,0:T(2,128)(2,1)S(1)}, u32[]{:S(2)}, u32[]{:S(2)}) %all-to-all-start) | async-done | bytes 262176 | tf_op jit(solution)/shard_map/all_to_all | solution.py:211
  39.1 11.8 %all-to-all-start.1 = ((bf16[32,2,2048]{2,1,0:T(2,128)(2,1)}), bf16[32,2,2048]{2,1,0:T(2,128)(2,1)S(1)}, u32[]{:S(2)}, u32[]{:S(2)}) async-start(bf16[32,2,2048]{2,1,0:T(2,128)(2,1)} %bitcast.12), calls=%async_computation.1 | async-start | bytes 524288 | tf_op jit(solution)/shard_map/all_to_all | solution.py:211
  50.9 0.1 slice.17
  51.0 0.1 slice.16
  51.1 0.3 maximum_convert_fusion
  51.4 0.4 reshape.35
  51.8 0.1 add_convert_fusion.refs_0_
  51.8 1.9 %collective-permute-start.3 = (bf16[64,2048]{1,0:T(8,128)(2,1)S(1)}, bf16[64,2048]{1,0:T(8,128)(2,1)S(1)}, u32[]{:S(2)}, u32[]{:S(2)}) collective-permute-start(bf16[64,2048]{1,0:T(8,128)(2,1)S(1)} %add_convert_fusion.refs_0_), channel_id=1, source_target_pairs={{0,256},{128,384},{256,0},{384,128},{1,257},{129,385},{257,1},{385... | collective-permute-start | bytes 786440 | tf_op jit(solution)/shard_map/ppermute | solution.py:221
  53.7 5.0 %collective-permute-start.2 = (bf16[64,2048]{1,0:T(8,128)(2,1)S(1)}, bf16[64,2048]{1,0:T(8,128)(2,1)S(1)}, u32[]{:S(2)}, u32[]{:S(2)}) collective-permute-start(bf16[64,2048]{1,0:T(8,128)(2,1)S(1)} %add_convert_fusion.refs_0_), channel_id=1, source_target_pairs={{0,128},{128,0},{256,384},{384,256},{1,129},{129,1},{257,385},{385... | collective-permute-start | bytes 786440 | tf_op jit(solution)/shard_map/ppermute | solution.py:221
  58.8 2.0 %collective-permute-done.3.refs_2_ = bf16[64,2048]{1,0:T(8,128)(2,1)S(1)} collective-permute-done((bf16[64,2048]{1,0:T(8,128)(2,1)S(1)}, bf16[64,2048]{1,0:T(8,128)(2,1)S(1)}, u32[]{:S(2)}, u32[]{:S(2)}) %collective-permute-start.3) | collective-permute-done | bytes 262176 | tf_op jit(solution)/shard_map/ppermute | solution.py:221
  60.8 5.2 %collective-permute-start.4 = (bf16[64,2048]{1,0:T(8,128)(2,1)S(1)}, bf16[64,2048]{1,0:T(8,128)(2,1)S(1)}, u32[]{:S(2)}, u32[]{:S(2)}) collective-permute-start(bf16[64,2048]{1,0:T(8,128)(2,1)S(1)} %collective-permute-done.3.refs_2_), channel_id=1, source_target_pairs={{0,128},{128,0},{256,384},{384,256},{1,129},{129,1},{257,385},{385... | collective-permute-start | bytes 786440 | tf_op jit(solution)/shard_map/ppermute | solution.py:221
  66.0 0.0 collective-permute-done.2.refs_1_
  66.0 1.1 %shard_map.59 = (bf16[256,2048]{1,0:T(8,128)(2,1)}, bf16[64,2048]{1,0:T(8,128)(2,1)S(1)}) custom-call(s32[1]{0:T(128)} %bitcast.1.rep_ref, bf16[256,2048]{1,0:T(8,128)(2,1)S(1)} %bitcast.27, bf16[64,2048]{1,0:T(8,128)(2,1)S(1)} %add_convert_fusion.refs_0_, bf16[64,2048]{1,0:T(8,128)(2,1)S(1)} %collective-permute-done.2.refs_1_, ...), custom_call_target="tpu_custom_call" | custom-call | bytes 131072 | tf_op jit(solution)/shard_map/pallas_call | solution.py:156
  67.1 0.0 collective-permute-done.4.copy_ref
  67.1 0.0 copy-start.1
  67.2 0.0 copy-start.2
  67.2 0.8 %shard_map.60 = bf16[256,2048]{1,0:T(8,128)(2,1)} custom-call(s32[1]{0:T(128)} %bitcast.place_ref, bf16[64,2048]{1,0:T(8,128)(2,1)S(1)} %get-tuple-element.14.shard_ref, bf16[64,2048]{1,0:T(8,128)(2,1)S(1)} %collective-permute-done.4.copy_ref, bf16[256,2048]{1,0:T(8,128)(2,1)} %get-tuple-element.15.before_ref), custom_call_target="tpu_custom_call", output_to_operand_aliasing={{}: (3, {})} | custom-call | bytes 65536 | tf_op jit(solution)/shard_map/pallas_call | solution.py:184
  68.0 0.0 all-to-all-done.1.total_ref
  68.0 0.2 copy-done.1
  68.2 0.2 copy-done.2
  68.4 1.1 %shard_map.61 = (f32[32,2,2048]{2,1,0:T(2,128)}, f32[32,2,2048]{2,1,0:T(2,128)}) custom-call(bf16[32,2,2048]{2,1,0:T(2,128)(2,1)S(1)} %all-to-all-done.1.total_ref, f32[32,2,2048]{2,1,0:T(2,128)S(1)} %bitcast.29, f32[32,2,2048]{2,1,0:T(2,128)S(1)} %bitcast.31), custom_call_target="tpu_custom_call" | custom-call | bytes 3145728 | tf_op jit(solution)/shard_map/pallas_call | solution.py:105
  (1 shorter events, 0.0 us)
Async XLA Ops:
  0.6 24.4 %copy-start = (bf16[1,256,2048]{2,1,0:T(8,128)(2,1)S(1)}, bf16[1,256,2048]{2,1,0:T(8,128)(2,1)}, u32[]{:S(2)}) copy-start(bf16[1,256,2048]{2,1,0:T(8,128)(2,1)} %param.3) | copy-start | bytes 3145732
  3.1 21.9 %collective-permute-start = (bf16[128,2048]{1,0:T(8,128)(2,1)}, bf16[128,2048]{1,0:T(8,128)(2,1)S(1)}, u32[]{:S(2)}, u32[]{:S(2)}) collective-permute-start(bf16[128,2048]{1,0:T(8,128)(2,1)} %get-tuple-element.12), channel_id=1, source_target_pairs={{0,256},{128,384},{256,0},{384,128},{1,257},{129,385},{257,1},{385... | collective-permute-start | bytes 1572872 | tf_op jit(solution)/shard_map/ppermute | solution.py:221
  7.1 32.0 %all-to-all-start = ((bf16[32,2,2048]{2,1,0:T(2,128)(2,1)}), bf16[32,2,2048]{2,1,0:T(2,128)(2,1)S(1)}, u32[]{:S(2)}, u32[]{:S(2)}) async-start(bf16[32,2,2048]{2,1,0:T(2,128)(2,1)} %get-tuple-element.11), calls=%async_computation | async-start | bytes 524288 | tf_op jit(solution)/shard_map/all_to_all | solution.py:211
  25.2 4.7 %collective-permute-start.1 = (bf16[64,2048]{1,0:T(8,128)(2,1)S(1)}, bf16[64,2048]{1,0:T(8,128)(2,1)}, u32[]{:S(2)}, u32[]{:S(2)}) collective-permute-start(bf16[64,2048]{1,0:T(8,128)(2,1)S(1)} %fusion), channel_id=1, source_target_pairs={{0,128},{128,0},{256,384},{384,256},{1,129},{129,1},{257,385},{385... | collective-permute-start | bytes 786440 | tf_op jit(solution)/shard_map/ppermute | solution.py:221
  39.1 28.9 %all-to-all-start.1 = ((bf16[32,2,2048]{2,1,0:T(2,128)(2,1)}), bf16[32,2,2048]{2,1,0:T(2,128)(2,1)S(1)}, u32[]{:S(2)}, u32[]{:S(2)}) async-start(bf16[32,2,2048]{2,1,0:T(2,128)(2,1)} %bitcast.12), calls=%async_computation.1 | async-start | bytes 524288 | tf_op jit(solution)/shard_map/all_to_all | solution.py:211
  51.8 8.9 %collective-permute-start.3 = (bf16[64,2048]{1,0:T(8,128)(2,1)S(1)}, bf16[64,2048]{1,0:T(8,128)(2,1)S(1)}, u32[]{:S(2)}, u32[]{:S(2)}) collective-permute-start(bf16[64,2048]{1,0:T(8,128)(2,1)S(1)} %add_convert_fusion.refs_0_), channel_id=1, source_target_pairs={{0,256},{128,384},{256,0},{384,128},{1,257},{129,385},{257,1},{385... | collective-permute-start | bytes 786440 | tf_op jit(solution)/shard_map/ppermute | solution.py:221
  53.7 12.2 %collective-permute-start.2 = (bf16[64,2048]{1,0:T(8,128)(2,1)S(1)}, bf16[64,2048]{1,0:T(8,128)(2,1)S(1)}, u32[]{:S(2)}, u32[]{:S(2)}) collective-permute-start(bf16[64,2048]{1,0:T(8,128)(2,1)S(1)} %add_convert_fusion.refs_0_), channel_id=1, source_target_pairs={{0,128},{128,0},{256,384},{384,256},{1,129},{129,1},{257,385},{385... | collective-permute-start | bytes 786440 | tf_op jit(solution)/shard_map/ppermute | solution.py:221
  60.8 6.4 %collective-permute-start.4 = (bf16[64,2048]{1,0:T(8,128)(2,1)S(1)}, bf16[64,2048]{1,0:T(8,128)(2,1)S(1)}, u32[]{:S(2)}, u32[]{:S(2)}) collective-permute-start(bf16[64,2048]{1,0:T(8,128)(2,1)S(1)} %collective-permute-done.3.refs_2_), channel_id=1, source_target_pairs={{0,128},{128,0},{256,384},{384,256},{1,129},{129,1},{257,385},{385... | collective-permute-start | bytes 786440 | tf_op jit(solution)/shard_map/ppermute | solution.py:221
  67.1 1.1 %copy-start.1 = (f32[32,1,2,2048]{3,2,1,0:T(2,128)S(1)}, f32[32,1,2,2048]{3,2,1,0:T(2,128)}, u32[]{:S(2)}) copy-start(f32[32,1,2,2048]{3,2,1,0:T(2,128)} %param.4) | copy-start | bytes 1572868
  67.2 1.3 %copy-start.2 = (f32[32,1,2,2048]{3,2,1,0:T(2,128)S(1)}, f32[32,1,2,2048]{3,2,1,0:T(2,128)}, u32[]{:S(2)}) copy-start(f32[32,1,2,2048]{3,2,1,0:T(2,128)} %param.5) | copy-start | bytes 1572868

commit v7 on v6

--- a/solution.py
+++ b/solution.py
@@ -86,7 +86,8 @@
 
 def update_kernel(total_ref, weights_ref, momentum_ref, outer_ref, out_momentum_ref, outer, out_momentum, sems):
     stores = []
-    for n, (place, index, length) in enumerate(segments(weights_ref.shape[0])):
+    runs = sorted(segments(weights_ref.shape[0]), key=lambda run: -run[2])
+    for n, (place, index, length) in enumerate(runs):
         rows = pl.ds(index, length)
         weights = weights_ref[rows]
         pseudo_grad = weights - 0.25 * total_ref[pl.ds(place, length)].astype(F32)

time: 70 us -> 70 us (level)
  no operation moved by 1% of the time
where the time goes in v7:
time: 70 us; the launch traced here: 69.5 us
  starting transfers between devices  49.2 us (70%)
  waiting for transfers between devices  9.92 us (14%)
  Pallas kernels  5.52 us (8%)
  other arithmetic  2.53 us (4%)
  local copies, waits for them, and re-layouts  1.41 us (2%)
  between operations  0.91 us (1%)
    all_to_all x2, starting transfers between devices, exchange(): lax.all_to_all(value, 'fsdp', split_axis=0, concat_axis=0, axis_index_gro...  29.7 us
    ppermute x5, starting transfers between devices, swap(): return lax.ppermute(value, 'rep', [(r, r ^ i) for r in range(replicas)])  19.5 us
    all_to_all x2, waiting for transfers between devices, exchange(): lax.all_to_all(value, 'fsdp', split_axis=0, concat_axis=0, axis_index_gro...  6.7 us
    ppermute x5, waiting for transfers between devices, swap(): return lax.ppermute(value, 'rep', [(r, r ^ i) for r in range(replicas)])  3.23 us
    pallas_call x1, Pallas kernels, state_and_other(): pl.pallas_call(first_kernel, in_specs=[SMEM, HBM, HBM, HBM], out_specs=[H...  2.48 us
  transfers between devices with their start and end apart: 7, of which 3 were waited for; matrix products, arithmetic and copies ran while one was open for 5% of the time, Pallas kernels for 3%

profile of v7, /device:TPU:1, one launch (start us, length us, event | category | flops | bytes accessed | tf_op | source)
XLA Modules:
  0.0 69.5 jit_solution(17691998928303346382)
XLA Ops:
  0.6 0.0 copy-start
  0.7 2.5 %shard_map.58 = (bf16[32,2,2048]{2,1,0:T(2,128)(2,1)}, bf16[128,2048]{1,0:T(8,128)(2,1)}) custom-call(s32[1]{0:T(128)} %bitcast.3.chip_ref, f32[32,2,2048]{2,1,0:T(2,128)} %bitcast.28, f32[32,2,2048]{2,1,0:T(2,128)} %bitcast.30, bf16[2,128,2048]{2,1,0:T(8,128)(2,1)} %bitcast.25), custom_call_target="tpu_custom_call" | custom-call | bytes 3145728 | tf_op jit(solution)/shard_map/pallas_call | solution.py:68
  3.1 3.9 %collective-permute-start = (bf16[128,2048]{1,0:T(8,128)(2,1)}, bf16[128,2048]{1,0:T(8,128)(2,1)S(1)}, u32[]{:S(2)}, u32[]{:S(2)}) collective-permute-start(bf16[128,2048]{1,0:T(8,128)(2,1)} %get-tuple-element.12), channel_id=1, source_target_pairs={{0,256},{128,384},{256,0},{384,128},{1,257},{129,385},{257,1},{385... | collective-permute-start | bytes 1572872 | tf_op jit(solution)/shard_map/ppermute | solution.py:222
  7.1 17.9 %all-to-all-start = ((bf16[32,2,2048]{2,1,0:T(2,128)(2,1)}), bf16[32,2,2048]{2,1,0:T(2,128)(2,1)S(1)}, u32[]{:S(2)}, u32[]{:S(2)}) async-start(bf16[32,2,2048]{2,1,0:T(2,128)(2,1)} %get-tuple-element.11), calls=%async_computation | async-start | bytes 524288 | tf_op jit(solution)/shard_map/all_to_all | solution.py:212
  25.0 0.0 collective-permute-done
  25.1 0.0 copy-done
  25.1 0.1 convert_add_fusion
  25.2 3.4 %collective-permute-start.1 = (bf16[64,2048]{1,0:T(8,128)(2,1)S(1)}, bf16[64,2048]{1,0:T(8,128)(2,1)}, u32[]{:S(2)}, u32[]{:S(2)}) collective-permute-start(bf16[64,2048]{1,0:T(8,128)(2,1)S(1)} %fusion), channel_id=1, source_target_pairs={{0,128},{128,0},{256,384},{384,256},{1,129},{129,1},{257,385},{385... | collective-permute-start | bytes 786440 | tf_op jit(solution)/shard_map/ppermute | solution.py:222
  28.7 1.3 %collective-permute-done.1 = bf16[64,2048]{1,0:T(8,128)(2,1)} collective-permute-done((bf16[64,2048]{1,0:T(8,128)(2,1)S(1)}, bf16[64,2048]{1,0:T(8,128)(2,1)}, u32[]{:S(2)}, u32[]{:S(2)}) %collective-permute-start.1) | collective-permute-done | bytes 262176 | tf_op jit(solution)/shard_map/ppermute | solution.py:222
  29.9 1.0 %fusion.1 = (bf16[64,2048]{1,0:T(8,128)(2,1)S(1)}, f32[64,2048]{1,0:T(8,128)S(1)}) fusion(bf16[64,2048]{1,0:T(8,128)(2,1)} %collective-permute-done.1, f32[2,64,2048]{2,1,0:T(8,128)S(1)} %bitcast.33, s32[]{:T(128)S(6)} %select_n.25), kind=kLoop, calls=%fused_computation.7 | loop fusion | flops 393216 | bytes 1572868 | tf_op jit(solution)/shard_map/convert_element_type | solution.py:234
  31.0 0.2 reshape_reshape.4
  31.2 0.1 slice.18
  31.2 0.1 slice.19
  31.4 1.0 %pad_maximum_fusion = bf16[2,16,2,2048]{3,2,1,0:T(2,128)(2,1)} fusion(bf16[2,11,2,2048]{3,2,1,0:T(2,128)(2,1)S(1)} %slice.19, bf16[2,5,2,2048]{3,2,1,0:T(2,128)(2,1)S(1)} %slice.18), kind=kLoop, calls=%fused_computation.6 | loop fusion | flops 131072 | bytes 524288 | tf_op jit(solution)/shard_map/concatenate | solution.py:218
  32.4 6.7 %all-to-all-done = bf16[32,2,2048]{2,1,0:T(2,128)(2,1)S(1)} async-done(((bf16[32,2,2048]{2,1,0:T(2,128)(2,1)}), bf16[32,2,2048]{2,1,0:T(2,128)(2,1)S(1)}, u32[]{:S(2)}, u32[]{:S(2)}) %all-to-all-start) | async-done | bytes 262176 | tf_op jit(solution)/shard_map/all_to_all | solution.py:212
  39.1 11.8 %all-to-all-start.1 = ((bf16[32,2,2048]{2,1,0:T(2,128)(2,1)}), bf16[32,2,2048]{2,1,0:T(2,128)(2,1)S(1)}, u32[]{:S(2)}, u32[]{:S(2)}) async-start(bf16[32,2,2048]{2,1,0:T(2,128)(2,1)} %bitcast.12), calls=%async_computation.1 | async-start | bytes 524288 | tf_op jit(solution)/shard_map/all_to_all | solution.py:212
  50.9 0.1 slice.17
  51.0 0.1 slice.16
  51.1 0.3 maximum_convert_fusion
  51.4 0.4 reshape.35
  51.8 0.1 add_convert_fusion.refs_0_
  51.8 1.9 %collective-permute-start.3 = (bf16[64,2048]{1,0:T(8,128)(2,1)S(1)}, bf16[64,2048]{1,0:T(8,128)(2,1)S(1)}, u32[]{:S(2)}, u32[]{:S(2)}) collective-permute-start(bf16[64,2048]{1,0:T(8,128)(2,1)S(1)} %add_convert_fusion.refs_0_), channel_id=1, source_target_pairs={{0,256},{128,384},{256,0},{384,128},{1,257},{129,385},{257,1},{385... | collective-permute-start | bytes 786440 | tf_op jit(solution)/shard_map/ppermute | solution.py:222
  53.7 5.0 %collective-permute-start.2 = (bf16[64,2048]{1,0:T(8,128)(2,1)S(1)}, bf16[64,2048]{1,0:T(8,128)(2,1)S(1)}, u32[]{:S(2)}, u32[]{:S(2)}) collective-permute-start(bf16[64,2048]{1,0:T(8,128)(2,1)S(1)} %add_convert_fusion.refs_0_), channel_id=1, source_target_pairs={{0,128},{128,0},{256,384},{384,256},{1,129},{129,1},{257,385},{385... | collective-permute-start | bytes 786440 | tf_op jit(solution)/shard_map/ppermute | solution.py:222
  58.8 2.0 %collective-permute-done.3.refs_2_ = bf16[64,2048]{1,0:T(8,128)(2,1)S(1)} collective-permute-done((bf16[64,2048]{1,0:T(8,128)(2,1)S(1)}, bf16[64,2048]{1,0:T(8,128)(2,1)S(1)}, u32[]{:S(2)}, u32[]{:S(2)}) %collective-permute-start.3) | collective-permute-done | bytes 262176 | tf_op jit(solution)/shard_map/ppermute | solution.py:222
  60.8 5.2 %collective-permute-start.4 = (bf16[64,2048]{1,0:T(8,128)(2,1)S(1)}, bf16[64,2048]{1,0:T(8,128)(2,1)S(1)}, u32[]{:S(2)}, u32[]{:S(2)}) collective-permute-start(bf16[64,2048]{1,0:T(8,128)(2,1)S(1)} %collective-permute-done.3.refs_2_), channel_id=1, source_target_pairs={{0,128},{128,0},{256,384},{384,256},{1,129},{129,1},{257,385},{385... | collective-permute-start | bytes 786440 | tf_op jit(solution)/shard_map/ppermute | solution.py:222
  66.0 0.0 collective-permute-done.2.refs_1_
  66.0 1.1 %shard_map.59 = (bf16[256,2048]{1,0:T(8,128)(2,1)}, bf16[64,2048]{1,0:T(8,128)(2,1)S(1)}) custom-call(s32[1]{0:T(128)} %bitcast.1.rep_ref, bf16[256,2048]{1,0:T(8,128)(2,1)S(1)} %bitcast.27, bf16[64,2048]{1,0:T(8,128)(2,1)S(1)} %add_convert_fusion.refs_0_, bf16[64,2048]{1,0:T(8,128)(2,1)S(1)} %collective-permute-done.2.refs_1_, ...), custom_call_target="tpu_custom_call" | custom-call | bytes 131072 | tf_op jit(solution)/shard_map/pallas_call | solution.py:157
  67.1 0.0 collective-permute-done.4.copy_ref
  67.1 0.0 copy-start.1
  67.2 0.0 copy-start.2
  67.2 0.8 %shard_map.60 = bf16[256,2048]{1,0:T(8,128)(2,1)} custom-call(s32[1]{0:T(128)} %bitcast.place_ref, bf16[64,2048]{1,0:T(8,128)(2,1)S(1)} %get-tuple-element.14.shard_ref, bf16[64,2048]{1,0:T(8,128)(2,1)S(1)} %collective-permute-done.4.copy_ref, bf16[256,2048]{1,0:T(8,128)(2,1)} %get-tuple-element.15.before_ref), custom_call_target="tpu_custom_call", output_to_operand_aliasing={{}: (3, {})} | custom-call | bytes 65536 | tf_op jit(solution)/shard_map/pallas_call | solution.py:185
  68.0 0.0 all-to-all-done.1.total_ref
  68.0 0.2 copy-done.1
  68.2 0.2 copy-done.2
  68.4 1.1 %shard_map.61 = (f32[32,2,2048]{2,1,0:T(2,128)}, f32[32,2,2048]{2,1,0:T(2,128)}) custom-call(bf16[32,2,2048]{2,1,0:T(2,128)(2,1)S(1)} %all-to-all-done.1.total_ref, f32[32,2,2048]{2,1,0:T(2,128)S(1)} %bitcast.29, f32[32,2,2048]{2,1,0:T(2,128)S(1)} %bitcast.31), custom_call_target="tpu_custom_call" | custom-call | bytes 3145728 | tf_op jit(solution)/shard_map/pallas_call | solution.py:106
  (1 shorter events, 0.0 us)
Async XLA Ops:
  0.6 24.4 %copy-start = (bf16[1,256,2048]{2,1,0:T(8,128)(2,1)S(1)}, bf16[1,256,2048]{2,1,0:T(8,128)(2,1)}, u32[]{:S(2)}) copy-start(bf16[1,256,2048]{2,1,0:T(8,128)(2,1)} %param.3) | copy-start | bytes 3145732
  3.1 21.9 %collective-permute-start = (bf16[128,2048]{1,0:T(8,128)(2,1)}, bf16[128,2048]{1,0:T(8,128)(2,1)S(1)}, u32[]{:S(2)}, u32[]{:S(2)}) collective-permute-start(bf16[128,2048]{1,0:T(8,128)(2,1)} %get-tuple-element.12), channel_id=1, source_target_pairs={{0,256},{128,384},{256,0},{384,128},{1,257},{129,385},{257,1},{385... | collective-permute-start | bytes 1572872 | tf_op jit(solution)/shard_map/ppermute | solution.py:222
  7.1 32.0 %all-to-all-start = ((bf16[32,2,2048]{2,1,0:T(2,128)(2,1)}), bf16[32,2,2048]{2,1,0:T(2,128)(2,1)S(1)}, u32[]{:S(2)}, u32[]{:S(2)}) async-start(bf16[32,2,2048]{2,1,0:T(2,128)(2,1)} %get-tuple-element.11), calls=%async_computation | async-start | bytes 524288 | tf_op jit(solution)/shard_map/all_to_all | solution.py:212
  25.2 4.7 %collective-permute-start.1 = (bf16[64,2048]{1,0:T(8,128)(2,1)S(1)}, bf16[64,2048]{1,0:T(8,128)(2,1)}, u32[]{:S(2)}, u32[]{:S(2)}) collective-permute-start(bf16[64,2048]{1,0:T(8,128)(2,1)S(1)} %fusion), channel_id=1, source_target_pairs={{0,128},{128,0},{256,384},{384,256},{1,129},{129,1},{257,385},{385... | collective-permute-start | bytes 786440 | tf_op jit(solution)/shard_map/ppermute | solution.py:222
  39.1 28.9 %all-to-all-start.1 = ((bf16[32,2,2048]{2,1,0:T(2,128)(2,1)}), bf16[32,2,2048]{2,1,0:T(2,128)(2,1)S(1)}, u32[]{:S(2)}, u32[]{:S(2)}) async-start(bf16[32,2,2048]{2,1,0:T(2,128)(2,1)} %bitcast.12), calls=%async_computation.1 | async-start | bytes 524288 | tf_op jit(solution)/shard_map/all_to_all | solution.py:212
  51.8 8.9 %collective-permute-start.3 = (bf16[64,2048]{1,0:T(8,128)(2,1)S(1)}, bf16[64,2048]{1,0:T(8,128)(2,1)S(1)}, u32[]{:S(2)}, u32[]{:S(2)}) collective-permute-start(bf16[64,2048]{1,0:T(8,128)(2,1)S(1)} %add_convert_fusion.refs_0_), channel_id=1, source_target_pairs={{0,256},{128,384},{256,0},{384,128},{1,257},{129,385},{257,1},{385... | collective-permute-start | bytes 786440 | tf_op jit(solution)/shard_map/ppermute | solution.py:222
  53.7 12.2 %collective-permute-start.2 = (bf16[64,2048]{1,0:T(8,128)(2,1)S(1)}, bf16[64,2048]{1,0:T(8,128)(2,1)S(1)}, u32[]{:S(2)}, u32[]{:S(2)}) collective-permute-start(bf16[64,2048]{1,0:T(8,128)(2,1)S(1)} %add_convert_fusion.refs_0_), channel_id=1, source_target_pairs={{0,128},{128,0},{256,384},{384,256},{1,129},{129,1},{257,385},{385... | collective-permute-start | bytes 786440 | tf_op jit(solution)/shard_map/ppermute | solution.py:222
  60.8 6.4 %collective-permute-start.4 = (bf16[64,2048]{1,0:T(8,128)(2,1)S(1)}, bf16[64,2048]{1,0:T(8,128)(2,1)S(1)}, u32[]{:S(2)}, u32[]{:S(2)}) collective-permute-start(bf16[64,2048]{1,0:T(8,128)(2,1)S(1)} %collective-permute-done.3.refs_2_), channel_id=1, source_target_pairs={{0,128},{128,0},{256,384},{384,256},{1,129},{129,1},{257,385},{385... | collective-permute-start | bytes 786440 | tf_op jit(solution)/shard_map/ppermute | solution.py:222
  67.1 1.1 %copy-start.1 = (f32[32,1,2,2048]{3,2,1,0:T(2,128)S(1)}, f32[32,1,2,2048]{3,2,1,0:T(2,128)}, u32[]{:S(2)}) copy-start(f32[32,1,2,2048]{3,2,1,0:T(2,128)} %param.4) | copy-start | bytes 1572868
  67.2 1.3 %copy-start.2 = (f32[32,1,2,2048]{3,2,1,0:T(2,128)S(1)}, f32[32,1,2,2048]{3,2,1,0:T(2,128)}, u32[]{:S(2)}) copy-start(f32[32,1,2,2048]{3,2,1,0:T(2,128)} %param.5) | copy-start | bytes 1572868
